TPU v7x, 256 devices: a whole 4x4x8 slice. The times are simulated.
256 devices in a mesh: grp: 2 (over core), reg: 128 (over y, x, z).
Axes of the slice: x: 4, y: 4, z: 8, core: 2. Of those that a mesh axis runs over, the one named last changes fastest.
Arguments:
- anchors: float32 [3, 16384], P(None, ('grp', 'reg')), may hold values from -3 to 3
- directions: float32 [3, 16384], P(None, ('grp', 'reg')), may hold values from -4 to 4
- targets: float32 [3, 16384], P(None, ('grp', 'reg')), may hold values from 0 to 1
- region_ids: int32 [16384, 4], P(('grp', 'reg')), may hold values from 0 to 255, all different within a row; in each aligned block of 64 rows (0 to 63, 64 to 127, ...) at most 2 rows name the same one
- sample_counts: int32 [16384, 4], P(('grp', 'reg')), may hold values from 1 to 8
- depth_index: int32 [16384, 4, 8], P(('grp', 'reg')), may hold values from 0 to 127
- frequencies: float32 [3, 128], replicated, may hold values from -6 to 6
- w_input: bfloat16 [256, 256, 256], P(('grp', 'reg')), may hold values from -0.375 to 0.375
- w_hidden: bfloat16 [256, 2, 256, 256], P(('grp', 'reg')), may hold values from -0.375 to 0.375
- w_head: bfloat16 [256, 256, 4], P(('grp', 'reg')), may hold values from -0.375 to 0.375
Outputs:
- colours: float32 [3, 16384], P(None, ('grp', 'reg'))
- grad_input: bfloat16 [256, 256, 256], P(('grp', 'reg'))
- grad_hidden: bfloat16 [256, 2, 256, 256], P(('grp', 'reg'))
- grad_head: bfloat16 [256, 256, 4], P(('grp', 'reg'))
Inputs may be any that keep to these rules, and one draw needn't show every extreme that they name: `region_ids`: within the rays of one device no region is named by more than 2 segments, a bound that some block reaches; the 4 segments of one ray name different regions.
All inputs are finite; a program needn't handle non-finite values.
Results may differ from a plain program's by a relative error of at most 0.015.
Values may be sent and summed in bfloat16 or wider, within the bound.
A program may use at most 64 MiB of HBM per device.

v0:
```python
import jax
import jax.numpy as jnp
from jax import lax
from jax.sharding import PartitionSpec as P

DEPTHS = 128


def depth_of(index):
    return 0.1 + (index.astype(jnp.float32) + 0.5) * (2.0 / DEPTHS)


def encode(anchor, direction, depth, frequencies):
    phases = None
    for column in range(3):
        position = anchor[..., column : column + 1] + depth * direction[..., column : column + 1]
        product_term = position[..., None] * frequencies[column]
        phases = product_term if phases is None else phases + product_term
    return jnp.concatenate([jnp.sin(phases), jnp.cos(phases)], axis=-1).astype(jnp.bfloat16)


def network(weights, encoded):
    first, middle, last = weights
    hidden = jax.nn.silu(jnp.dot(encoded, first, preferred_element_type=jnp.float32)).astype(
        jnp.bfloat16
    )
    for layer_index in range(middle.shape[0]):
        hidden = jax.nn.silu(
            jnp.dot(hidden, middle[layer_index], preferred_element_type=jnp.float32)
        ).astype(jnp.bfloat16)
    return jnp.dot(hidden, last, preferred_element_type=jnp.float32)


def composite(values, live):
    sigma = jax.nn.softplus(values[..., 0])
    colour = jax.nn.sigmoid(values[..., 1:4])
    opacity = live * (1.0 - jnp.exp(-0.5 * sigma))
    through = jnp.cumprod(1.0 - opacity, axis=-1)
    before = jnp.concatenate([jnp.ones_like(through[..., :1]), through[..., :-1]], axis=-1)
    seg_colour = jnp.sum((before * opacity)[..., None] * colour, axis=-2)
    return jnp.concatenate([seg_colour, through[..., -1:]], axis=-1)


def render(segments):
    through = jnp.cumprod(segments[..., 3], axis=-1)
    before = jnp.concatenate([jnp.ones_like(through[:, :1]), through[:, :-1]], axis=-1)
    return jnp.sum(before[..., None] * segments[..., :3], axis=1) + through[:, -1:]


def per_device(
    anchors,
    directions,
    targets,
    region_ids,
    sample_counts,
    depth_index,
    frequencies,
    w_input,
    w_hidden,
    w_head,
):
    groups = lax.axis_size("grp")
    owners_count = lax.axis_size("reg")
    devices = groups * owners_count
    ray_count, seg_count = region_ids.shape
    samples = depth_index.shape[2]
    capacity = max(2, 2 * ray_count * seg_count // devices)
    features = w_input.shape[1]
    slot_total = devices * capacity
    buffer_shape = (groups, owners_count, capacity)
    region_flat = region_ids.reshape(-1)
    owners = jnp.arange(devices, dtype=jnp.int32)
    onehot = (region_flat[:, None] == owners[None, :]).astype(jnp.int32)
    ranking = jnp.cumsum(onehot, axis=0) - onehot
    slot_index = jnp.sum(ranking * onehot, axis=1)
    position = region_flat * capacity + slot_index
    segment_anchor = jnp.repeat(anchors.T, seg_count, axis=0)
    segment_direction = jnp.repeat(directions.T, seg_count, axis=0)
    counts_flat = sample_counts.reshape(-1)
    depth_flat = depth_of(depth_index).reshape(-1, samples)
    sample_iota = jnp.arange(samples, dtype=jnp.int32)
    live_flat = (sample_iota[None, :] < counts_flat[:, None]).astype(jnp.float32)
    encoded = encode(segment_anchor, segment_direction, depth_flat, frequencies)
    send_encoded = (
        jnp.zeros((slot_total, samples, features), jnp.bfloat16).at[position].set(encoded)
    )
    send_live = (
        jnp.zeros((slot_total, samples), jnp.bfloat16)
        .at[position]
        .set(live_flat.astype(jnp.bfloat16))
    )
    recv_encoded, recv_live = (
        lax.all_to_all(
            lax.all_to_all(
                send_encoded.reshape(buffer_shape + (samples, features)),
                "grp",
                split_axis=0,
                concat_axis=0,
                tiled=True,
            ),
            "reg",
            split_axis=1,
            concat_axis=1,
            tiled=True,
        ),
        lax.all_to_all(
            lax.all_to_all(
                send_live.reshape(buffer_shape + (samples,)),
                "grp",
                split_axis=0,
                concat_axis=0,
                tiled=True,
            ),
            "reg",
            split_axis=1,
            concat_axis=1,
            tiled=True,
        ),
    )
    owner_rows = recv_encoded.reshape(-1, features)
    params = (w_input[0], w_hidden[0], w_head[0])
    raw, network_pull = jax.vjp(lambda weights: network(weights, owner_rows), params)
    raw = raw.reshape(-1, samples, 4)
    back_raw = lax.all_to_all(
        lax.all_to_all(
            raw.reshape(buffer_shape + (samples, 4)), "grp", split_axis=0, concat_axis=0, tiled=True
        ),
        "reg",
        split_axis=1,
        concat_axis=1,
        tiled=True,
    )
    segment_raw = back_raw.reshape(-1, samples, 4)[position]

    def render_local(values):
        return render(composite(values, live_flat).reshape(ray_count, seg_count, 4))

    colours, render_pull = jax.vjp(render_local, segment_raw)
    segment_grad = render_pull(colours - targets.T)[0]
    send_grad = jnp.zeros((slot_total, samples, 4), jnp.float32).at[position].set(segment_grad)
    owner_grad = lax.all_to_all(
        lax.all_to_all(
            send_grad.reshape(buffer_shape + (samples, 4)),
            "grp",
            split_axis=0,
            concat_axis=0,
            tiled=True,
        ),
        "reg",
        split_axis=1,
        concat_axis=1,
        tiled=True,
    )
    owner_grad = owner_grad.reshape(-1, 4)
    gradients = network_pull(owner_grad)[0]
    return (colours.T, gradients[0][None], gradients[1][None], gradients[2][None])


def solution(mesh):
    return jax.shard_map(
        per_device,
        mesh=mesh,
        in_specs=(
            P(None, ("grp", "reg")),
            P(None, ("grp", "reg")),
            P(None, ("grp", "reg")),
            P(("grp", "reg"), None),
            P(("grp", "reg"), None),
            P(("grp", "reg"), None, None),
            P(),
            P(("grp", "reg"), None, None),
            P(("grp", "reg"), None, None, None),
            P(("grp", "reg"), None, None),
        ),
        out_specs=(
            P(None, ("grp", "reg")),
            P(("grp", "reg"), None, None),
            P(("grp", "reg"), None, None, None),
            P(("grp", "reg"), None, None),
        ),
        check_vma=False,
    )
```

profile of v0, /device:TPU:1, one launch (start us, length us, event | category | flops | bytes accessed | tf_op | source)
XLA Modules:
  0.0 215.2 jit_solution(7611693021541773562)
XLA Ops:
  0.6 0.7 broadcast_multiply_fusion.1
  1.4 0.8 copy.131
  2.7 0.2 fusion.19
  3.0 0.8 slice_bitcast_fusion.4
  3.8 0.7 multiply_add_fusion.4
  4.6 0.8 broadcast_in_dim.53
  5.5 0.8 broadcast_in_dim.52
  6.6 0.3 multiply_add_fusion.3
  6.9 4.2 %sine_convert_fusion = (bf16[256,8,128]{2,1,0:T(8,128)(2,1)S(1)}, bf16[256,8,128]{2,1,0:T(8,128)(2,1)S(1)}) fusion(f32[128]{0:T(128)S(1)} %get-tuple-element.58, f32[256,8]{1,0:T(8,128)S(1)} %get-tuple-element.15, f32[128]{0:T(128)S(1)} %get-tuple-element.59, f32[256,8]{1,0:T(8,128)S(1)} %get-tuple-element.16, f32[128]{0:T(128)S(1)} %get-tuple-element.57, ...), kind=kLoop, calls=%fused_computation.39 | loop fusion | flops 1835008 | bytes 1074688 | tf_op jit(solution)/shard_map/convert
  11.4 6.9 %scatter_fusion = bf16[512,8,256]{2,1,0:T(8,128)(2,1)S(1)} fusion(bf16[512,8,256]{2,1,0:T(8,128)(2,1)S(1)} %broadcast_in_dim.51, s32[256]{0:T(256)S(1)} %bitcast.146, bf16[256,8,256]{2,1,0:T(8,128)(2,1)S(1)} %pad_maximum_fusion), kind=kCustom, calls=%fused_computation.1 | custom fusion | bytes 3146752 | tf_op jit(solution)/shard_map/scatter | solution.py:85
  18.4 8.3 %all_to_all.30 = bf16[2,128,2,8,256]{4,3,2,1,0:T(8,128)(2,1)S(1)} all-to-all(bf16[2,128,2,8,256]{4,3,2,1,0:T(8,128)(2,1)S(1)} %bitcast.136), channel_id=1, replica_groups=mesh['grp'=2,'reg'=128] {'grp'}, dimensions={0} | all-to-all | bytes 4194304 | tf_op jit(solution)/shard_map/all_to_all | solution.py:94
  26.6 0.3 copy.136
  27.0 66.5 %all_to_all.31 = bf16[2,128,2,8,256]{4,3,2,0,1:T(8,128)(2,1)S(1)} all-to-all(bf16[2,128,2,8,256]{4,3,2,0,1:T(8,128)(2,1)S(1)} %copy.136), channel_id=1, replica_groups=mesh['grp'=2,'reg'=128] {'reg'}, dimensions={1} | all-to-all | bytes 4194304 | tf_op jit(solution)/shard_map/all_to_all | solution.py:93
  93.6 0.7 fusion.30
  94.3 0.6 copy-done.1
  94.9 2.0 copy-done.2
  96.9 1.2 fusion.28
  98.1 3.5 %multiply_convert_fusion = (bf16[4096,256]{1,0:T(8,128)(2,1)S(1)}, f32[4096,256]{1,0:T(8,128)}) fusion(bf16[1,2,256,256]{3,2,1,0:T(8,128)(2,1)S(1)} %copy-done.7, f32[4096,256]{1,0:T(8,128)S(1)} %fusion.28), kind=kOutput, calls=%fused_computation.22 | convolution fusion | flops 547356672 | bytes 10616832 | tf_op jit(solution)/shard_map/jvp()/dot_general | solution.py:29
  101.7 4.7 %fusion.49 = f32[2,128,2,8,4]{3,4,2,1,0:T(4,128)S(1)} fusion(bf16[2,128,2,8,256]{4,3,2,1,0:T(8,128)(2,1)S(1)} %bitcast.133, bf16[1,256,4]{1,2,0:T(4,128)(2,1)S(1)} %copy-done.3), kind=kOutput, calls=%fused_computation.131 | convolution fusion | flops 8388608 | bytes 2164736 | tf_op jit(solution)/shard_map/jvp()/dot_general | solution.py:31
  106.4 0.4 copy.138
  106.8 5.9 %all_to_all.32 = f32[2,128,2,8,4]{1,3,4,2,0:T(8,128)S(1)} all-to-all(f32[2,128,2,8,4]{1,3,4,2,0:T(8,128)S(1)} %copy.138), channel_id=1, replica_groups=mesh['grp'=2,'reg'=128] {'grp'}, dimensions={0} | all-to-all | bytes 131072 | tf_op jit(solution)/shard_map/all_to_all | solution.py:125
  112.7 0.6 copy.139
  113.3 1.8 reshape.256
  115.1 6.1 %all-to-all-start.3 = ((f32[128,1,128]{2,1,0:T(1,128)}), f32[128,1,128]{2,1,0:T(1,128)S(1)}, u32[]{:S(2)}, u32[]{:S(2)}) async-start(f32[128,1,128]{2,1,0:T(1,128)} %reshape.256), calls=%async_computation.3 | async-start | bytes 131072 | tf_op jit(solution)/shard_map/all_to_all | solution.py:124
  121.5 10.3 %all-to-all-done.3 = f32[128,1,128]{2,1,0:T(1,128)S(1)} async-done(((f32[128,1,128]{2,1,0:T(1,128)}), f32[128,1,128]{2,1,0:T(1,128)S(1)}, u32[]{:S(2)}, u32[]{:S(2)}) %all-to-all-start.3) | async-done | bytes 65568 | tf_op jit(solution)/shard_map/all_to_all | solution.py:124
  131.8 0.5 broadcast.288
  132.3 0.8 reduce.2
  133.1 1.2 reshape.257
  134.3 0.5 copy.140
  134.9 1.7 copy.141
  136.6 2.2 %gather_fusion = f32[256,8,4]{1,2,0:T(4,128)S(1)} fusion(f32[512,8,4]{1,2,0:T(4,128)} %copy.141, s32[1024]{0:T(1024)S(1)} %pad_clamp_fusion), kind=kCustom, calls=%fused_computation | custom fusion | bytes 66560 | tf_op jit(solution)/shard_map/gather | solution.py:133
  141.0 0.6 fusion.60
  143.2 1.0 copy.145
  144.4 16.3 %scatter_fusion.1 = f32[512,8,4]{1,2,0:T(4,128)S(1)} fusion(f32[512,8,4]{1,2,0:T(4,128)S(1)} %broadcast_in_dim.54, s32[256]{0:T(256)S(1)} %bitcast.148, f32[256,8,4]{1,2,0:T(4,128)} %copy.145), kind=kCustom, calls=%fused_computation.2 | custom fusion | bytes 99328 | tf_op jit(solution)/shard_map/scatter | solution.py:140
  160.7 0.4 copy.146
  161.1 4.8 %all_to_all.33 = bf16[2,128,2,8,4]{1,3,4,2,0:T(8,128)(2,1)S(1)} all-to-all(bf16[2,128,2,8,4]{1,3,4,2,0:T(8,128)(2,1)S(1)} %copy.146), channel_id=1, replica_groups=mesh['grp'=2,'reg'=128] {'grp'}, dimensions={0} | all-to-all | bytes 65536 | tf_op jit(solution)/shard_map/all_to_all | solution.py:142
  165.9 0.5 copy.147
  166.4 25.1 %all_to_all.34 = bf16[2,128,2,8,4]{3,2,0,4,1:T(2,128)(2,1)S(1)} all-to-all(bf16[2,128,2,8,4]{3,2,0,4,1:T(2,128)(2,1)S(1)} %copy.147), channel_id=1, replica_groups=mesh['grp'=2,'reg'=128] {'reg'}, dimensions={1} | all-to-all | bytes 65536 | tf_op jit(solution)/shard_map/all_to_all | solution.py:141
  191.5 0.4 copy.148
  191.9 0.6 reshape.229
  192.5 4.1 %fusion = bf16[4096,256]{1,0:T(8,128)(2,1)S(1)} fusion(f32[4096,256]{1,0:T(8,128)} %get-tuple-element.61, bf16[4096,4]{0,1:T(4,128)(2,1)S(1)} %reshape.229, bf16[1,256,4]{1,2,0:T(4,128)(2,1)S(1)} %copy-done.3), kind=kOutput, calls=%fused_computation.15 | convolution fusion | flops 19922944 | bytes 6326272 | tf_op jit(solution)/shard_map/transpose(jvp())/dot_general | solution.py:31
  196.6 1.3 copy-done.12
  197.9 3.2 %fusion.2 = bf16[4096,256]{1,0:T(8,128)(2,1)} fusion(f32[4096,256]{1,0:T(8,128)S(1)} %copy-done.10, bf16[4096,256]{1,0:T(8,128)(2,1)S(1)} %fusion, bf16[1,2,256,256]{3,2,1,0:T(8,128)(2,1)S(1)} %copy-done.8), kind=kOutput, calls=%fused_computation.17 | convolution fusion | flops 548405248 | bytes 8519680 | tf_op jit(solution)/shard_map/transpose(jvp())/dot_general | solution.py:29
  201.2 6.1 %fusion.15 = bf16[1,256,256]{2,1,0:T(8,128)(2,1)} fusion(bf16[4096,256]{1,0:T(8,128)(2,1)} %bitcast.135, f32[4096,256]{1,0:T(8,128)} %copy-done.2, bf16[4096,256]{1,0:T(8,128)(2,1)} %fusion.2, bf16[1,2,256,256]{3,2,1,0:T(8,128)(2,1)S(1)} %copy-done.8), kind=kOutput, calls=%fused_computation.34 | convolution fusion | flops 1085276160 | bytes 8650752 | tf_op jit(solution)/shard_map/transpose(jvp())/dot_general | solution.py:24
  207.2 4.6 %fusion.14 = bf16[1,256,256]{2,1,0:T(8,128)(2,1)S(1)} fusion(bf16[4096,256]{1,0:T(8,128)(2,1)} %fusion.2, f32[4096,256]{1,0:T(8,128)} %copy-done.2), kind=kOutput, calls=%fused_computation.33 | convolution fusion | flops 542113792 | bytes 6422528 | tf_op jit(solution)/shard_map/transpose(jvp())/dot_general | solution.py:29
  212.0 1.6 fusion.13
  213.5 1.0 fusion.18
  214.5 0.7 add_bitcast_fusion
  (136 shorter events, 5.7 us)
Async XLA Ops:
  0.6 93.0 %copy-start = (bf16[1,256,256]{2,1,0:T(8,128)(2,1)S(1)}, bf16[1,256,256]{2,1,0:T(8,128)(2,1)}, u32[]{:S(2)}) copy-start(bf16[1,256,256]{2,1,0:T(8,128)(2,1)} %param.17) | copy-start | bytes 393220
  93.6 1.3 copy-start.1
  93.6 3.3 %copy-start.7 = (bf16[1,2,256,256]{3,2,1,0:T(8,128)(2,1)S(1)}, bf16[1,2,256,256]{3,2,1,0:T(8,128)(2,1)}, u32[]{:S(2)}) copy-start(bf16[1,2,256,256]{3,2,1,0:T(8,128)(2,1)} %param.18) | copy-start | bytes 786436
  94.9 2.0 copy-start.2
  98.1 3.5 %copy-start.9 = (f32[4096,256]{1,0:T(8,128)}, f32[4096,256]{1,0:T(8,128)S(1)}, u32[]{:S(2)}) copy-start(f32[4096,256]{1,0:T(8,128)S(1)} %fusion.28) | copy-start | bytes 12582916
  98.1 3.5 %copy-start.3 = (bf16[1,256,4]{1,2,0:T(4,128)(2,1)S(1)}, bf16[1,256,4]{1,2,0:T(4,128)(2,1)}, u32[]{:S(2)}) copy-start(bf16[1,256,4]{1,2,0:T(4,128)(2,1)} %param.19) | copy-start | bytes 6148
  101.7 19.6 %copy-start.5 = (s32[64,4]{0,1:T(4,128)S(1)}, s32[64,4]{0,1:T(4,128)}, u32[]{:S(2)}) copy-start(s32[64,4]{0,1:T(4,128)} %param.14) | copy-start | bytes 3076
  115.1 16.7 %all-to-all-start.3 = ((f32[128,1,128]{2,1,0:T(1,128)}), f32[128,1,128]{2,1,0:T(1,128)S(1)}, u32[]{:S(2)}, u32[]{:S(2)}) async-start(f32[128,1,128]{2,1,0:T(1,128)} %reshape.256), calls=%async_computation.3 | async-start | bytes 131072 | tf_op jit(solution)/shard_map/all_to_all | solution.py:124
  134.9 6.1 %copy-start.6 = (f32[3,64]{1,0:T(4,128)S(1)}, f32[3,64]{1,0:T(4,128)}, u32[]{:S(2)}) copy-start(f32[3,64]{1,0:T(4,128)} %param.12) | copy-start | bytes 2308
  134.9 7.4 %copy-start.4 = (pred[2]{0:T(512)(128)(4,1)S(1)}, pred[2]{0:T(512)(128)(4,1)}, u32[]{:S(2)}) copy-start(pred[2]{0:T(512)(128)(4,1)} %constant.54.clone.1) | copy-start | bytes 10
  192.5 5.5 %copy-start.8 = (bf16[1,2,256,256]{3,2,1,0:T(8,128)(2,1)S(1)}, bf16[1,2,256,256]{3,2,1,0:T(8,128)(2,1)}, u32[]{:S(2)}) copy-start(bf16[1,2,256,256]{3,2,1,0:T(8,128)(2,1)} %param.18) | copy-start | bytes 786436
  192.5 5.5 %copy-start.10 = (f32[4096,256]{1,0:T(8,128)S(1)}, f32[4096,256]{1,0:T(8,128)}, u32[]{:S(2)}) copy-start(f32[4096,256]{1,0:T(8,128)} %copy-done.9) | copy-start | bytes 12582916
  196.6 1.4 copy-start.12
  207.2 4.6 %copy-start.11 = (f32[4096,256]{1,0:T(8,128)S(1)}, f32[4096,256]{1,0:T(8,128)}, u32[]{:S(2)}) copy-start(f32[4096,256]{1,0:T(8,128)} %copy-done.9) | copy-start | bytes 12582916
  207.2 4.7 %copy-start.13 = (bf16[4096,256]{1,0:T(8,128)(2,1)S(1)}, bf16[4096,256]{1,0:T(8,128)(2,1)}, u32[]{:S(2)}) copy-start(bf16[4096,256]{1,0:T(8,128)(2,1)} %copy-done.12) | copy-start | bytes 6291460
where the time goes:
time: 217 us; the launch traced here: 215 us
  blocking collectives  111 us (51%)
  local copies, waits for them, and re-layouts  46.1 us (21%)
  matrix products  30.6 us (14%)
  waiting for transfers between devices  10.3 us (5%)
  other arithmetic  10.2 us (5%)
  starting transfers between devices  6.15 us (3%)
    all_to_all x1, blocking collectives, per_device(): lax.all_to_all(lax.all_to_all(send_encoded.reshape(buffer_shape + (sample...  66.5 us
    all_to_all x1, blocking collectives, per_device(): lax.all_to_all(lax.all_to_all(send_grad.reshape(buffer_shape + (samples,...  25.1 us
    scatter x1, local copies, waits for them, and re-layouts, per_device(): jnp.zeros((slot_total, samples, 4), jnp.float32).at[position]  16.3 us
    dot_general x5, matrix products, network(): jnp.dot(hidden, middle[layer_index], preferred_element_type=jnp.float32)  14.1 us
    all_to_all x1, waiting for transfers between devices, per_device(): lax.all_to_all(lax.all_to_all(raw.reshape(buffer_shape + (samples, 4)), '...  10.3 us
    dot_general x3, matrix products, network(): return jnp.dot(hidden, last, preferred_element_type=jnp.float32)  9.75 us
    unnamed x37, local copies, waits for them, and re-layouts  8.3 us
    all_to_all x1, blocking collectives, per_device(): lax.all_to_all(send_encoded.reshape(buffer_shape + (samples, features)),...  8.29 us
  transfers between devices with their start and end apart: 1, of which 1 were waited for; matrix products, arithmetic and copies ran while one was open for 0% of the time, Pallas kernels for 0%

commit v1 on v0

v1 whole, which is shorter than its diff:
```python
import functools
import math

import jax
import jax.numpy as jnp
from jax import lax
from jax.experimental import pallas as pl
from jax.experimental.pallas import tpu as pltpu
from jax.sharding import PartitionSpec as P

DEPTHS = 128
CHIPS_Z = 8
LANES = 128
MESH = pl.DeviceIdType.MESH
F32 = jnp.float32
BF16 = jnp.bfloat16

SIN = (6.283182621002197, -41.34142303466797, 81.59620666503906, -76.58030700683594,
       41.2061653137207, -12.272321701049805)
COS = (1.0, -19.73920440673828, 64.93911743164062, -85.45016479492188, 60.16783142089844,
       -25.968313217163086, 6.529609680175781)


def horner(coefficients, x):
    total = jnp.full_like(x, coefficients[-1])
    for value in coefficients[-2::-1]:
        total = total * x + value
    return total


def dot(a, b):
    return jnp.dot(a, b, preferred_element_type=F32)


def dot_nt(a, b):
    return lax.dot_general(a, b, (((1,), (1,)), ((), ())), preferred_element_type=F32)


def pieces(x):
    high = x.astype(BF16).astype(F32)
    rest = x - high
    middle = rest.astype(BF16).astype(F32)
    return high, middle, (rest - middle).astype(BF16).astype(F32)


def copies(source, target, rows, count, me, device, sends, receives):
    def outgoing(step):
        peer = lax.rem(me + step, count)
        return pltpu.make_async_remote_copy(
            src_ref=source.at[pl.ds(pl.multiple_of(peer * rows, rows), rows)],
            dst_ref=target.at[pl.ds(pl.multiple_of(me * rows, rows), rows)],
            send_sem=sends.at[peer],
            recv_sem=receives.at[me],
            device_id=device(peer),
            device_id_type=MESH,
        )

    def incoming(step):
        peer = lax.rem(me + step, count)
        part = target.at[pl.ds(pl.multiple_of(peer * rows, rows), rows)]
        return pltpu.make_async_remote_copy(
            src_ref=part,
            dst_ref=part,
            send_sem=sends.at[peer],
            recv_sem=receives.at[peer],
            device_id=device(peer),
            device_id_type=MESH,
        )

    return outgoing, incoming


def each(count, act):
    def body(step, carry):
        act(step)
        return carry

    lax.fori_loop(1, count, body, 0)


def exchange(source, target, rows, count, me, device, sends, receives):
    outgoing, incoming = copies(source, target, rows, count, me, device, sends, receives)
    each(count, lambda step: outgoing(step).start())
    own = pl.ds(pl.multiple_of(me * rows, rows), rows)
    target[own, :] = source[own, :]
    return (
        lambda: each(count, lambda step: incoming(step).wait_recv()),
        lambda: each(count, lambda step: outgoing(step).wait_send()),
    )


def turned(source, target, major, minor):
    for index in range(minor):
        target[index * major : (index + 1) * major, :] = source[
            pl.ds(index, major, stride=minor), :
        ]


def kernel(
    sizes,
    anchors, directions, targets, regions, counts, depths, frequencies, w_in, w_hid, w_head,
    colours, g_in, g_hid, g_head,
    send1, mid1, turn1, last1, send2, mid2, turn2, last2, send3, mid3, turn3, last3,
    rows_s, words_s, words_b, onehot, target_s, freq_s, slots_s, phase0, phase1, depth_s, head_s,
    raw_s, graw_s, cot_b, w1, wh, w1t, w2t, w3t, w2, w3, wot, wo, encoded, hidden, slope,
    acc1, acc2, acc3, acc4, sends, receives, local,
):
    groups, regs, zn, rays, segs, samples = sizes
    n = groups * regs
    near, far = groups * zn, regs // zn
    slots = 2 * n
    width = segs * LANES
    features = w_hid.shape[-1]
    freqs = features // 2

    grp = lax.axis_index("grp").astype(jnp.int32)
    reg = lax.axis_index("reg").astype(jnp.int32)
    me_far = lax.div(reg, zn)
    me_z = lax.rem(reg, zn)
    me_near = grp * zn + me_z

    def near_device(index):
        return (lax.div(index, zn), me_far * zn + lax.rem(index, zn))

    def far_device(index):
        return (grp, index * zn + me_z)

    barrier = pltpu.get_barrier_semaphore()

    def greet(count, me, device):
        def act(step):
            pl.semaphore_signal(
                barrier, inc=1, device_id=device(lax.rem(me + step, count)), device_id_type=MESH
            )

        each(count, act)

    greet(near, me_near, near_device)
    greet(far, me_far, far_device)

    load_in = pltpu.make_async_copy(w_in.at[0], w1, local.at[0])
    load_hid = pltpu.make_async_copy(w_hid.at[0], wh, local.at[1])
    load_in.start()
    load_hid.start()

    ids = regions[...]
    in_group = lax.rem(ids, regs)
    place = (lax.div(ids, regs) * zn + lax.rem(in_group, zn)) * far + lax.div(in_group, zn)
    rows_s[...] = jnp.full(rows_s.shape, -1, jnp.int32)
    words_s[...] = jnp.zeros(words_s.shape, F32)
    for k in range(segs):
        part = slice(k * LANES, k * LANES + rays)
        rows_s[0:1, part] = place[k : k + 1]
        both = jnp.concatenate([anchors[...], directions[...]], axis=0)
        high, middle, low = pieces(both)
        words_s[0:6, part] = high
        words_s[6:12, part] = middle
        words_s[12:18, part] = low
        words_s[18:19, part] = counts[k : k + 1].astype(F32)
        words_s[24 : 24 + samples, part] = depths[k].astype(F32)
    row_of = rows_s[0:1, :]
    match = row_of == lax.broadcasted_iota(jnp.int32, (n, width), 0)
    number = lax.broadcasted_iota(jnp.int32, (n, width), 1)
    last = jnp.max(jnp.where(match, number, -1), axis=1, keepdims=True)
    first_slot = number == last
    onehot[:, 0:width] = jnp.where(first_slot, 1.0, 0.0).astype(BF16)
    onehot[:, width:] = jnp.where(match & jnp.logical_not(first_slot), 1.0, 0.0).astype(BF16)
    words_b[...] = jnp.zeros(words_b.shape, BF16)
    packed = words_s[...].astype(BF16)
    words_b[0:32, 0:width] = packed
    words_b[32:64, width:] = packed
    send1[...] = dot_nt(onehot[...], words_b[...])

    pl.semaphore_wait(barrier, near + far - 2)

    wait_near1, sent_near1 = exchange(
        send1, mid1, far, near, me_near, near_device, sends.at[0], receives.at[0]
    )
    load_in.wait()
    load_hid.wait()
    w1t[...] = (w1[...].astype(F32) * 0.5).T.astype(BF16)
    half2 = wh[0].astype(F32) * 0.5
    w2[...] = half2.astype(BF16)
    w2t[...] = half2.T.astype(BF16)
    half3 = wh[1].astype(F32) * 0.5
    w3[...] = half3.astype(BF16)
    w3t[...] = half3.T.astype(BF16)
    wait_near1()
    turned(mid1, turn1, near, far)
    wait_far1, sent_far1 = exchange(
        turn1, last1, near, far, me_far, far_device, sends.at[1], receives.at[1]
    )
    head_s[...] = jnp.zeros(head_s.shape, F32)
    head_s[0:4, :] = w_head[...].astype(F32)
    wot[...] = head_s[...].astype(BF16)
    wo[...] = (head_s[...] * 0.5).T.astype(BF16)
    freq_s[...] = jnp.zeros(freq_s.shape, F32)
    freq_s[0:3, :] = frequencies[...] * (1.0 / (2.0 * math.pi))
    columns = freq_s[...].T
    send2[...] = jnp.zeros(send2.shape, F32)
    send3[...] = jnp.zeros(send3.shape, F32)
    graw_s[...] = jnp.zeros(graw_s.shape, F32)
    cot_b[...] = jnp.zeros(cot_b.shape, BF16)
    target_s[...] = jnp.zeros(target_s.shape, F32)
    target_s[0:3, 0:rays] = targets[...]
    acc1[...] = jnp.zeros(acc1.shape, F32)
    acc2[...] = jnp.zeros(acc2.shape, F32)
    acc3[...] = jnp.zeros(acc3.shape, F32)
    acc4[...] = jnp.zeros(acc4.shape, F32)
    wait_far1()

    words = last1[...].T
    slots_s[:, 0:n] = words[0:32]
    slots_s[:, n:] = words[32:64]
    geometry = (slots_s[0:6, :] + slots_s[6:12, :]) + slots_s[12:18, :]
    base = jnp.zeros((freqs, slots), F32)
    rate = jnp.zeros((freqs, slots), F32)
    for c in range(3):
        base = base + columns[:, c : c + 1] * geometry[c : c + 1]
        rate = rate + columns[:, c : c + 1] * geometry[3 + c : 4 + c]
    phase0[...] = base
    phase1[...] = rate
    depth_s[...] = 0.1 + (slots_s[24 : 24 + samples, :] + 0.5) * (2.0 / DEPTHS)
    live = jnp.where(
        lax.broadcasted_iota(jnp.int32, (samples, slots), 0).astype(F32) < slots_s[18:19, :],
        1.0, 0.0,
    )

    def layer(index, j, weights, x):
        z = dot(weights, x)
        t = jnp.tanh(z)
        h = z + z * t
        hidden[index, j] = h.astype(BF16)
        slope[index, j] = ((1.0 + h) + t * (1.0 - h)).astype(BF16)
        return h.astype(BF16)

    def forward(j, carry):
        turns = phase0[...] + depth_s[pl.ds(j, 1), :] * phase1[...]
        r = turns - jnp.round(turns)
        square = r * r
        x = jnp.concatenate([r * horner(SIN, square), horner(COS, square)], axis=0).astype(BF16)
        encoded[j] = x
        x = layer(0, j, w1t[...], x)
        x = layer(1, j, w2t[...], x)
        x = layer(2, j, w3t[...], x)
        raw = dot(wot[...], x)
        for k in range(4):
            raw_s[k, pl.ds(j, 1), :] = raw[k : k + 1]
        return carry

    lax.fori_loop(0, samples, forward, 0)

    density = raw_s[0]
    small = jnp.exp(-jnp.abs(density))
    softplus = jnp.maximum(density, 0.0) + jnp.log1p(small)
    clear = jnp.exp(-0.5 * softplus)
    alpha = live * (1.0 - clear)
    keep = 1.0 - alpha
    tone = [jax.nn.sigmoid(raw_s[1 + c]) for c in range(3)]
    through = jnp.ones((1, slots), F32)
    befores = []
    for i in range(samples):
        befores.append(through)
        through = through * keep[i : i + 1]
    before = jnp.concatenate(befores, axis=0)
    weight = before * alpha
    seg = [jnp.sum(weight * tone[c], axis=0, keepdims=True) for c in range(3)] + [through]
    answer = jnp.concatenate(
        [part[:, 0:n] for part in seg] + [part[:, n:] for part in seg], axis=0
    )
    send2[:, 0:8] = answer.T

    wait_far2, sent_far2 = exchange(
        send2, mid2, near, far, me_far, far_device, sends.at[2], receives.at[2]
    )
    d_density = 0.5 * live * clear * jnp.where(density >= 0.0, 1.0, small) / (1.0 + small)
    d_tone = [weight * t * (1.0 - t) for t in tone]
    wait_far2()
    turned(mid2, turn2, far, near)
    wait_near2, sent_near2 = exchange(
        turn2, last2, far, near, me_near, near_device, sends.at[3], receives.at[3]
    )
    wait_near2()

    values = last2[...].T[0:8]
    high, middle, low = pieces(values)
    blank = jnp.zeros((4, n), F32)
    left = jnp.concatenate([high[0:4], middle[0:4], low[0:4], blank], axis=0).astype(BF16)
    right = jnp.concatenate([high[4:8], middle[4:8], low[4:8], blank], axis=0).astype(BF16)
    found = dot(left, onehot[:, 0:width]) + dot(right, onehot[:, width:])
    found = (found[0:4] + found[4:8]) + found[8:12]
    arrive = [jnp.ones((1, LANES), F32)]
    total = jnp.zeros((3, LANES), F32)
    parts = []
    for k in range(segs):
        part = found[:, k * LANES : (k + 1) * LANES]
        parts.append(part)
        total = total + arrive[k] * part[0:3]
        arrive.append(arrive[k] * part[3:4])
    total = total + arrive[segs]
    colours[...] = total[:, 0:rays]
    error = total - target_s[0:3, :]
    behind = jnp.sum(error, axis=0, keepdims=True)
    for k in range(segs - 1, -1, -1):
        part = parts[k]
        cotangent = jnp.concatenate([arrive[k] * error, arrive[k] * behind], axis=0)
        behind = jnp.sum(error * part[0:3], axis=0, keepdims=True) + part[3:4] * behind
        stack = jnp.concatenate(
            list(pieces(cotangent)) + [jnp.zeros((4, LANES), F32)], axis=0
        ).astype(BF16)
        cot_b[0:16, k * LANES : (k + 1) * LANES] = stack
        cot_b[16:32, width + k * LANES : width + (k + 1) * LANES] = stack
    send3[:, 0:32] = dot_nt(onehot[...], cot_b[...])

    wait_near3, sent_near3 = exchange(
        send3, mid3, far, near, me_near, near_device, sends.at[4], receives.at[4]
    )
    wait_near3()
    turned(mid3, turn3, near, far)
    wait_far3, sent_far3 = exchange(
        turn3, last3, near, far, me_far, far_device, sends.at[5], receives.at[5]
    )
    wait_far3()

    words = last3[...].T[0:32]
    given = jnp.concatenate(
        [(words[0:4] + words[4:8]) + words[8:12], (words[16:20] + words[20:24]) + words[24:28]],
        axis=1,
    )
    gain = given[0:1] * tone[0] + given[1:2] * tone[1] + given[2:3] * tone[2]
    after = given[3:4]
    backs = []
    for i in range(samples - 1, -1, -1):
        backs.append(befores[i] * (gain[i : i + 1] - after))
        after = alpha[i : i + 1] * gain[i : i + 1] + keep[i : i + 1] * after
    d_raw = [jnp.concatenate(backs[::-1], axis=0) * d_density]
    d_raw += [given[c : c + 1] * d_tone[c] for c in range(3)]
    for j in range(samples):
        for k in range(4):
            graw_s[j, k : k + 1, :] = d_raw[k][j : j + 1]

    def backward(j, carry):
        g = graw_s[j].astype(BF16)
        h3 = hidden[2, j]
        acc4[...] += dot_nt(g, h3)
        g = (dot(wo[...], g) * slope[2, j].astype(F32)).astype(BF16)
        acc3[...] += dot_nt(hidden[1, j], g)
        g = (dot(w3[...], g) * slope[1, j].astype(F32)).astype(BF16)
        acc2[...] += dot_nt(hidden[0, j], g)
        g = (dot(w2[...], g) * slope[0, j].astype(F32)).astype(BF16)
        acc1[...] += dot_nt(encoded[j], g)
        return carry

    lax.fori_loop(0, samples, backward, 0)
    g_in[0] = acc1[...].astype(BF16)
    g_hid[0, 0] = acc2[...].astype(BF16)
    g_hid[0, 1] = acc3[...].astype(BF16)
    g_head[...] = acc4[0:4, :].astype(BF16)

    for sent in (sent_near1, sent_far1, sent_far2, sent_near2, sent_near3, sent_far3):
        sent()


def per_device(
    anchors, directions, targets, region_ids, sample_counts, depth_index, frequencies,
    w_input, w_hidden, w_head,
):
    groups, regs = lax.axis_size("grp"), lax.axis_size("reg")
    rays, segs = region_ids.shape
    samples = depth_index.shape[2]
    width = w_input.shape[1]
    zn = min(CHIPS_Z, regs)
    n = groups * regs
    slots = 2 * n
    near, far = groups * zn, regs // zn
    peers = max(near, far)
    lanes = segs * LANES
    board = [pltpu.VMEM((n, LANES), F32)] * 12
    square = (width, width)
    scratch = board + [
        pltpu.VMEM((8, lanes), jnp.int32),
        pltpu.VMEM((32, lanes), F32),
        pltpu.VMEM((LANES, 2 * lanes), BF16),
        pltpu.VMEM((n, 2 * lanes), BF16),
        pltpu.VMEM((8, LANES), F32),
        pltpu.VMEM((8, width // 2), F32),
        pltpu.VMEM((32, slots), F32),
        pltpu.VMEM((width // 2, slots), F32),
        pltpu.VMEM((width // 2, slots), F32),
        pltpu.VMEM((samples, slots), F32),
        pltpu.VMEM((16, width), F32),
        pltpu.VMEM((4, samples, slots), F32),
        pltpu.VMEM((samples, 16, slots), F32),
        pltpu.VMEM((32, 2 * lanes), BF16),
        pltpu.VMEM(square, BF16),
        pltpu.VMEM((2,) + square, BF16),
        pltpu.VMEM(square, BF16),
        pltpu.VMEM(square, BF16),
        pltpu.VMEM(square, BF16),
        pltpu.VMEM(square, BF16),
        pltpu.VMEM(square, BF16),
        pltpu.VMEM((16, width), BF16),
        pltpu.VMEM((width, 16), BF16),
        pltpu.VMEM((samples, width, slots), BF16),
        pltpu.VMEM((3, samples, width, slots), BF16),
        pltpu.VMEM((3, samples, width, slots), BF16),
        pltpu.VMEM(square, F32),
        pltpu.VMEM(square, F32),
        pltpu.VMEM(square, F32),
        pltpu.VMEM((16, width), F32),
        pltpu.SemaphoreType.DMA((6, peers)),
        pltpu.SemaphoreType.DMA((6, peers)),
        pltpu.SemaphoreType.DMA((2,)),
    ]
    vmem = pl.BlockSpec(memory_space=pltpu.VMEM)
    whole = pl.BlockSpec(memory_space=pl.ANY)
    colours, g_in, g_hid, g_head = pl.pallas_call(
        functools.partial(kernel, (groups, regs, zn, rays, segs, samples)),
        out_shape=(
            jax.ShapeDtypeStruct((3, rays), F32),
            jax.ShapeDtypeStruct(w_input.shape, BF16),
            jax.ShapeDtypeStruct(w_hidden.shape, BF16),
            jax.ShapeDtypeStruct((4, width), BF16),
        ),
        in_specs=[vmem] * 7 + [whole, whole, vmem],
        out_specs=[vmem] * 4,
        scratch_shapes=scratch,
        compiler_params=pltpu.CompilerParams(
            collective_id=0, has_side_effects=True, vmem_limit_bytes=48 * 1024 * 1024
        ),
        name="radiance_step",
    )(
        anchors, directions, targets, region_ids.T, sample_counts.T,
        depth_index.transpose(1, 2, 0), frequencies, w_input, w_hidden, w_head[0].T,
    )
    return colours, g_in, g_hid, g_head.T[None]


def solution(mesh):
    both = ("grp", "reg")
    return jax.shard_map(
        per_device,
        mesh=mesh,
        in_specs=(
            P(None, both), P(None, both), P(None, both), P(both, None), P(both, None),
            P(both, None, None), P(), P(both, None, None), P(both, None, None, None),
            P(both, None, None),
        ),
        out_specs=(
            P(None, both), P(both, None, None), P(both, None, None, None), P(both, None, None),
        ),
        check_vma=False,
    )
```

time: 217 us -> 73.1 us (0.34)
  blocking collectives: 111 us -> 0 us
  Pallas kernels: 0 us -> 63.6 us
  local copies, waits for them, and re-layouts: 46.1 us -> 8.5 us
  matrix products: 30.6 us -> 0 us
  waiting for transfers between devices: 10.3 us -> 0 us
  other arithmetic: 10.2 us -> 0 us
  starting transfers between devices: 6.15 us -> 0 us
    all_to_all x5 -> x0, blocking collectives: 111 us -> none  [the longest x1 66.5 us: per_device(): lax.all_to_all(lax.all_to_all(send_encoded.reshape(buffer_shape + (sample...]
    pallas_call x0 -> x1, Pallas kernels: none -> 63.6 us  [per_device(): pl.pallas_call(functools.partial(kernel, (groups, regs, zn, rays, segs, s...]
    dot_general x10 -> x0, matrix products: 30.6 us -> none  [the longest x5 14.1 us: network(): jnp.dot(hidden, middle[layer_index], preferred_element_type=jnp.float32)]
    scatter x2 -> x0, local copies, waits for them, and re-layouts: 23.2 us -> none  [the longest x1 16.3 us: per_device(): jnp.zeros((slot_total, samples, 4), jnp.float32).at[position]]
    all_to_all x1 -> x0, waiting for transfers between devices: 10.3 us -> none  [per_device(): lax.all_to_all(lax.all_to_all(raw.reshape(buffer_shape + (samples, 4)), '...]
    all_to_all x1 -> x0, starting transfers between devices: 6.15 us -> none  [per_device(): lax.all_to_all(lax.all_to_all(raw.reshape(buffer_shape + (samples, 4)), '...]
    another operation x4 -> x0, other arithmetic: 4.49 us -> none
    reshape x8 -> x0, local copies, waits for them, and re-layouts: 3.23 us -> none  [the longest x1 1.67 us: per_device(): segment_raw = back_raw.reshape(-1, samples, 4)[position]]
  transfers between devices with their start and end apart: 1 -> 0, of which waited for: 1 -> 0; matrix products, arithmetic and copies ran while one was open for 0% -> 0% of each run, Pallas kernels for 0% -> 0%
where the time goes in v1:
time: 73.1 us; the launch traced here: 72.8 us
  Pallas kernels  63.6 us (87%)
  local copies, waits for them, and re-layouts  8.5 us (12%)
    pallas_call x1, Pallas kernels, per_device(): pl.pallas_call(functools.partial(kernel, (groups, regs, zn, rays, segs, s...  63.6 us
    unnamed x24, local copies, waits for them, and re-layouts  8.5 us

profile of v1, /device:TPU:1, one launch (start us, length us, event | category | flops | bytes accessed | tf_op | source)
XLA Modules:
  0.0 72.8 jit_solution(7210359833441764193)
XLA Ops:
  0.6 0.0 copy-start.5
  0.6 0.0 copy-start.4
  0.7 0.0 copy-start.3
  0.7 0.7 copy-done.5
  1.3 0.0 copy-done.4
  1.3 0.0 copy-done.3
  1.3 0.0 copy-start
  1.4 0.9 %copy-done = bf16[1,2,256,256]{3,2,1,0:T(8,128)(2,1)S(1)} copy-done((bf16[1,2,256,256]{3,2,1,0:T(8,128)(2,1)S(1)}, bf16[1,2,256,256]{3,2,1,0:T(8,128)(2,1)}, u32[]{:S(2)}) %copy-start) | copy-done | bytes 262168
  2.3 0.0 copy-start.1
  2.3 0.9 %copy-done.1 = bf16[1,256,256]{2,1,0:T(8,128)(2,1)S(1)} copy-done((bf16[1,256,256]{2,1,0:T(8,128)(2,1)S(1)}, bf16[1,256,256]{2,1,0:T(8,128)(2,1)}, u32[]{:S(2)}) %copy-start.1) | copy-done | bytes 131096
  3.2 0.0 copy-start.2
  3.2 0.7 copy-done.2
  3.9 0.0 copy-start.6
  3.9 0.7 copy-done.6
  4.6 0.0 copy-start.7
  4.6 0.7 copy-done.7
  5.3 0.0 copy-start.8
  5.3 0.7 copy-done.8
  6.0 0.0 copy-start.9
  6.0 0.7 copy-done.9
  6.7 63.6 %radiance_step.1 = (f32[3,64]{1,0:T(4,128)S(1)}, bf16[1,256,256]{2,1,0:T(8,128)(2,1)S(1)}, bf16[1,2,256,256]{3,2,1,0:T(8,128)(2,1)S(1)}, bf16[4,256]{1,0:T(4,128)(2,1)S(1)}) custom-call(f32[3,64]{1,0:T(4,128)S(1)} %copy-done.3, f32[3,64]{1,0:T(4,128)S(1)} %copy-done.4, f32[3,64]{1,0:T(4,128)S(1)} %copy-done.5, s32[4,64]{1,0:T(4,128)S(1)} %bitcast.10, ...), custom_call_target="tpu_custom_call" | custom-call | tf_op jit(solution)/shard_map/radiance_step/pallas_call | solution.py:417
  70.3 0.6 copy.18
  70.9 0.7 copy.19
  71.5 0.7 copy.20
  72.2 0.6 copy.21
Async XLA Ops:
  0.6 0.7 copy-start.5
  0.6 0.7 copy-start.4
  0.7 0.7 copy-start.3
  1.3 0.9 %copy-start = (bf16[1,2,256,256]{3,2,1,0:T(8,128)(2,1)S(1)}, bf16[1,2,256,256]{3,2,1,0:T(8,128)(2,1)}, u32[]{:S(2)}) copy-start(bf16[1,2,256,256]{3,2,1,0:T(8,128)(2,1)} %w_hid.1) | copy-start | bytes 786436
  2.3 0.9 %copy-start.1 = (bf16[1,256,256]{2,1,0:T(8,128)(2,1)S(1)}, bf16[1,256,256]{2,1,0:T(8,128)(2,1)}, u32[]{:S(2)}) copy-start(bf16[1,256,256]{2,1,0:T(8,128)(2,1)} %w_in.1) | copy-start | bytes 393220
  3.2 0.7 copy-start.2
  3.9 0.7 copy-start.6
  4.6 0.7 copy-start.7
  5.3 0.7 copy-start.8
  6.0 0.7 copy-start.9

commit v2 on v1

v2 whole, which is shorter than its diff:
```python
import functools
import math

import jax
import jax.numpy as jnp
from jax import lax
from jax.experimental import pallas as pl
from jax.experimental.pallas import tpu as pltpu
from jax.sharding import PartitionSpec as P

DEPTHS = 128
CHIPS_Z = 8
VMEM_BYTES = 64 * 1024 * 1024
LANES = 128
MESH = pl.DeviceIdType.MESH
F32 = jnp.float32
BF16 = jnp.bfloat16

SIN = (6.283182621002197, -41.34142303466797, 81.59620666503906, -76.58030700683594,
       41.2061653137207, -12.272321701049805)
COS = (1.0, -19.73920440673828, 64.93911743164062, -85.45016479492188, 60.16783142089844,
       -25.968313217163086, 6.529609680175781)


def horner(coefficients, x):
    total = jnp.full_like(x, coefficients[-1])
    for value in coefficients[-2::-1]:
        total = total * x + value
    return total


def dot(a, b):
    return jnp.dot(a, b, preferred_element_type=F32)


def dot_nt(a, b):
    return lax.dot_general(a, b, (((1,), (1,)), ((), ())), preferred_element_type=F32)


def pieces(x):
    high = x.astype(BF16).astype(F32)
    rest = x - high
    middle = rest.astype(BF16).astype(F32)
    return high, middle, (rest - middle).astype(BF16).astype(F32)


def exchange(source, target, rows, count, me, device, send, receive):
    def part(ref, index):
        return ref.at[pl.ds(pl.multiple_of(index * rows, rows), rows)]

    for step in range(1, count):
        peer = lax.rem(me + step, count)
        pltpu.make_async_remote_copy(
            src_ref=part(source, peer),
            dst_ref=part(target, me),
            send_sem=send,
            recv_sem=receive,
            device_id=device(peer),
            device_id_type=MESH,
        ).start()
    own = pl.ds(pl.multiple_of(me * rows, rows), rows)
    target[own, :] = source[own, :]
    others = pl.ds(0, (count - 1) * rows)
    everything = pltpu.make_async_remote_copy(
        src_ref=source.at[others],
        dst_ref=target.at[others],
        send_sem=send,
        recv_sem=receive,
        device_id=device(lax.rem(me + 1, count)),
        device_id_type=MESH,
    )
    return everything.wait_recv, everything.wait_send


def turned(source, loose, target, major, minor):
    loose[...] = source[...].astype(F32)
    for index in range(minor):
        target[index * major : (index + 1) * major, :] = loose[
            pl.ds(index, major, stride=minor), :
        ].astype(BF16)


def staged(stages, count):
    for step in range(count + stages - 1):
        for stage in range(stages):
            if 0 <= step - stage < count:
                yield stage, step - stage


def kernel(
    sizes,
    *refs,
):
    arguments, results = refs[:10], refs[10:14]
    (
    send1, mid1, turn1, last1, send2, mid2, turn2, last2, send3, mid3, turn3, last3,
    loose, rows_s, words_s, words_b, onehot, target_s, freq_s, slots_s, phase0, phase1, depth_s, head_s,
    raw_s, graw_s, cot_b, w1t, w2t, w3t, w2, w3, wot, wo, encoded, hidden, slope, cotangents,
    acc1, acc2, acc3, acc4, colours, g_in, g_hid, g_head, sends, receives, local,
    ) = refs[24:]
    held = refs[14:24]
    anchors, directions, targets, regions, counts, depths, frequencies, w1, wh, w_head = held
    made = (colours, g_in, g_hid, g_head)
    groups, regs, zn, rays, segs, samples = sizes
    loads = [
        pltpu.make_async_copy(argument, place, local.at[index])
        for index, (argument, place) in enumerate(zip(arguments, held))
    ]
    for load in loads:
        load.start()
    n = groups * regs
    near, far = groups * zn, regs // zn
    slots = 2 * n
    width = segs * LANES
    features = wh.shape[-1]
    freqs = features // 2

    grp = lax.axis_index("grp").astype(jnp.int32)
    reg = lax.axis_index("reg").astype(jnp.int32)
    me_far = lax.div(reg, zn)
    me_z = lax.rem(reg, zn)
    me_near = grp * zn + me_z

    def near_device(index):
        return (lax.div(index, zn), me_far * zn + lax.rem(index, zn))

    def far_device(index):
        return (grp, index * zn + me_z)

    barrier = pltpu.get_barrier_semaphore()

    for count, me, device in ((near, me_near, near_device), (far, me_far, far_device)):
        for step in range(1, count):
            pl.semaphore_signal(
                barrier, inc=1, device_id=device(lax.rem(me + step, count)), device_id_type=MESH
            )
    for index in (0, 1, 3, 4, 5):
        loads[index].wait()

    ids = regions[...]
    in_group = lax.rem(ids, regs)
    place = (lax.div(ids, regs) * zn + lax.rem(in_group, zn)) * far + lax.div(in_group, zn)
    rows_s[...] = jnp.full(rows_s.shape, -1, jnp.int32)
    words_s[...] = jnp.zeros(words_s.shape, F32)
    for k in range(segs):
        part = slice(k * LANES, k * LANES + rays)
        rows_s[0:1, part] = place[k : k + 1]
        both = jnp.concatenate([anchors[...], directions[...]], axis=0)
        high, middle, low = pieces(both)
        words_s[0:6, part] = high
        words_s[6:12, part] = middle
        words_s[12:18, part] = low
        words_s[18:19, part] = counts[k : k + 1].astype(F32)
        words_s[24 : 24 + samples, part] = depths[k].astype(F32)
    row_of = rows_s[0:1, :]
    match = row_of == lax.broadcasted_iota(jnp.int32, (n, width), 0)
    number = lax.broadcasted_iota(jnp.int32, (n, width), 1)
    last = jnp.max(jnp.where(match, number, -1), axis=1, keepdims=True)
    first_slot = number == last
    onehot[:, 0:width] = jnp.where(first_slot, 1.0, 0.0).astype(BF16)
    onehot[:, width:] = jnp.where(match & jnp.logical_not(first_slot), 1.0, 0.0).astype(BF16)
    words_b[...] = jnp.zeros(words_b.shape, BF16)
    packed = words_s[...].astype(BF16)
    words_b[0:32, 0:width] = packed
    words_b[32:64, width:] = packed
    send1[...] = dot_nt(onehot[...], words_b[...]).astype(BF16)

    pl.semaphore_wait(barrier, near + far - 2)

    wait_near1, sent_near1 = exchange(
        send1, mid1, far, near, me_near, near_device, sends.at[0], receives.at[0]
    )
    for index in (2, 6, 7, 8, 9):
        loads[index].wait()
    w1t[...] = (w1[0].astype(F32) * 0.5).T.astype(BF16)
    half2 = wh[0, 0].astype(F32) * 0.5
    w2[...] = half2.astype(BF16)
    w2t[...] = half2.T.astype(BF16)
    half3 = wh[0, 1].astype(F32) * 0.5
    w3[...] = half3.astype(BF16)
    w3t[...] = half3.T.astype(BF16)
    wait_near1()
    turned(mid1, loose, turn1, near, far)
    wait_far1, sent_far1 = exchange(
        turn1, last1, near, far, me_far, far_device, sends.at[1], receives.at[1]
    )
    head_s[...] = jnp.zeros(head_s.shape, F32)
    head_s[0:4, :] = w_head[...].astype(F32)
    wot[...] = head_s[...].astype(BF16)
    wo[...] = (head_s[...] * 0.5).T.astype(BF16)
    freq_s[...] = jnp.zeros(freq_s.shape, F32)
    freq_s[0:3, :] = frequencies[...] * (1.0 / (2.0 * math.pi))
    columns = freq_s[...].T
    send2[...] = jnp.zeros(send2.shape, BF16)
    send3[...] = jnp.zeros(send3.shape, BF16)
    graw_s[...] = jnp.zeros(graw_s.shape, F32)
    cot_b[...] = jnp.zeros(cot_b.shape, BF16)
    target_s[...] = jnp.zeros(target_s.shape, F32)
    target_s[0:3, 0:rays] = targets[...]
    wait_far1()

    words = last1[...].astype(F32).T
    slots_s[:, 0:n] = words[0:32]
    slots_s[:, n:] = words[32:64]
    geometry = (slots_s[0:6, :] + slots_s[6:12, :]) + slots_s[12:18, :]
    base = jnp.zeros((freqs, slots), F32)
    rate = jnp.zeros((freqs, slots), F32)
    for c in range(3):
        base = base + columns[:, c : c + 1] * geometry[c : c + 1]
        rate = rate + columns[:, c : c + 1] * geometry[3 + c : 4 + c]
    phase0[...] = base
    phase1[...] = rate
    depth_s[...] = 0.1 + (slots_s[24 : 24 + samples, :] + 0.5) * (2.0 / DEPTHS)
    live = jnp.where(
        lax.broadcasted_iota(jnp.int32, (samples, slots), 0).astype(F32) < slots_s[18:19, :],
        1.0, 0.0,
    )

    layers = (w1t, w2t, w3t)
    for stage, j in staged(5, samples):
        if stage == 0:
            turns = phase0[...] + depth_s[j : j + 1, :] * phase1[...]
            r = turns - jnp.round(turns)
            square = r * r
            encoded[j, 0:freqs] = (r * horner(SIN, square)).astype(BF16)
            encoded[j, freqs:] = horner(COS, square).astype(BF16)
        elif stage < 4:
            z = dot(layers[stage - 1][...], encoded[j] if stage == 1 else hidden[stage - 2, j])
            t = jnp.tanh(z)
            h = z + z * t
            hidden[stage - 1, j] = h.astype(BF16)
            slope[stage - 1, j] = ((1.0 + h) + t * (1.0 - h)).astype(BF16)
        else:
            raw = dot(wot[...], hidden[2, j])
            for k in range(4):
                raw_s[k, j : j + 1, :] = raw[k : k + 1]

    density = raw_s[0]
    small = jnp.exp(-jnp.abs(density))
    softplus = jnp.maximum(density, 0.0) + jnp.log1p(small)
    clear = jnp.exp(-0.5 * softplus)
    alpha = live * (1.0 - clear)
    keep = 1.0 - alpha
    tone = [jax.nn.sigmoid(raw_s[1 + c]) for c in range(3)]
    through = jnp.ones((1, slots), F32)
    befores = []
    for i in range(samples):
        befores.append(through)
        through = through * keep[i : i + 1]
    before = jnp.concatenate(befores, axis=0)
    weight = before * alpha
    seg = [jnp.sum(weight * tone[c], axis=0, keepdims=True) for c in range(3)] + [through]
    answer = jnp.concatenate(seg, axis=0)
    blank = jnp.zeros((4, slots), F32)
    answer = jnp.concatenate(list(pieces(answer)) + [blank], axis=0)
    answer = jnp.concatenate([answer[:, 0:n], answer[:, n:]], axis=0)
    send2[:, 0:32] = answer.T.astype(BF16)

    wait_far2, sent_far2 = exchange(
        send2, mid2, near, far, me_far, far_device, sends.at[2], receives.at[2]
    )
    d_density = 0.5 * live * clear * jnp.where(density >= 0.0, 1.0, small) / (1.0 + small)
    d_tone = [weight * t * (1.0 - t) for t in tone]
    wait_far2()
    turned(mid2, loose, turn2, far, near)
    wait_near2, sent_near2 = exchange(
        turn2, last2, far, near, me_near, near_device, sends.at[3], receives.at[3]
    )
    wait_near2()

    values = last2[...].astype(F32).T[0:32].astype(BF16)
    found = dot(values[0:16], onehot[:, 0:width]) + dot(values[16:32], onehot[:, width:])
    found = (found[0:4] + found[4:8]) + found[8:12]
    arrive = [jnp.ones((1, LANES), F32)]
    total = jnp.zeros((3, LANES), F32)
    parts = []
    for k in range(segs):
        part = found[:, k * LANES : (k + 1) * LANES]
        parts.append(part)
        total = total + arrive[k] * part[0:3]
        arrive.append(arrive[k] * part[3:4])
    total = total + arrive[segs]
    colours[...] = total[:, 0:rays]
    error = total - target_s[0:3, :]
    behind = jnp.sum(error, axis=0, keepdims=True)
    for k in range(segs - 1, -1, -1):
        part = parts[k]
        cotangent = jnp.concatenate([arrive[k] * error, arrive[k] * behind], axis=0)
        behind = jnp.sum(error * part[0:3], axis=0, keepdims=True) + part[3:4] * behind
        stack = jnp.concatenate(
            list(pieces(cotangent)) + [jnp.zeros((4, LANES), F32)], axis=0
        ).astype(BF16)
        cot_b[0:16, k * LANES : (k + 1) * LANES] = stack
        cot_b[16:32, width + k * LANES : width + (k + 1) * LANES] = stack
    send3[:, 0:32] = dot_nt(onehot[...], cot_b[...]).astype(BF16)

    wait_near3, sent_near3 = exchange(
        send3, mid3, far, near, me_near, near_device, sends.at[4], receives.at[4]
    )
    wait_near3()
    turned(mid3, loose, turn3, near, far)
    wait_far3, sent_far3 = exchange(
        turn3, last3, near, far, me_far, far_device, sends.at[5], receives.at[5]
    )
    wait_far3()

    words = last3[...].astype(F32).T[0:32]
    given = jnp.concatenate(
        [(words[0:4] + words[4:8]) + words[8:12], (words[16:20] + words[20:24]) + words[24:28]],
        axis=1,
    )
    gain = given[0:1] * tone[0] + given[1:2] * tone[1] + given[2:3] * tone[2]
    after = given[3:4]
    backs = []
    for i in range(samples - 1, -1, -1):
        backs.append(befores[i] * (gain[i : i + 1] - after))
        after = alpha[i : i + 1] * gain[i : i + 1] + keep[i : i + 1] * after
    d_raw = [jnp.concatenate(backs[::-1], axis=0) * d_density]
    d_raw += [given[c : c + 1] * d_tone[c] for c in range(3)]
    for j in range(samples):
        for k in range(4):
            graw_s[j, k : k + 1, :] = d_raw[k][j : j + 1]

    backs = (wo, w3, w2)
    inputs = (lambda j: hidden[1, j], lambda j: hidden[0, j], lambda j: encoded[j])
    totals = (acc3, acc2, acc1)

    def gather(total, j, term):
        if j == 0:
            total[...] = term
        else:
            total[...] += term

    for stage, j in staged(4, samples):
        if stage == 0:
            gather(acc4, j, dot_nt(graw_s[j].astype(BF16), hidden[2, j]))
        if stage < 3:
            g = graw_s[j].astype(BF16) if stage == 0 else cotangents[stage - 1, j]
            g = dot(backs[stage][...], g) * slope[2 - stage, j].astype(F32)
            cotangents[stage, j] = g.astype(BF16)
        if stage > 0:
            gather(totals[stage - 1], j, dot_nt(inputs[stage - 1](j), cotangents[stage - 1, j]))

    g_in[0] = acc1[...].astype(BF16)
    g_hid[0, 0] = acc2[...].astype(BF16)
    g_hid[0, 1] = acc3[...].astype(BF16)
    g_head[...] = acc4[0:4, :].astype(BF16)
    stores = [
        pltpu.make_async_copy(place, result, local.at[10 + index])
        for index, (place, result) in enumerate(zip(made, results))
    ]
    for store in stores:
        store.start()
    for store in stores:
        store.wait()

    for sent in (sent_near1, sent_far1, sent_far2, sent_near2, sent_near3, sent_far3):
        sent()


def hand_over(*refs):
    moves = [
        pltpu.make_async_copy(refs[index], refs[4 + index], refs[8].at[index])
        for index in range(4)
    ]
    for move in moves:
        move.start()
    for move in moves:
        move.wait()


def per_device(
    anchors, directions, targets, region_ids, sample_counts, depth_index, frequencies,
    w_input, w_hidden, w_head,
):
    groups, regs = lax.axis_size("grp"), lax.axis_size("reg")
    rays, segs = region_ids.shape
    samples = depth_index.shape[2]
    width = w_input.shape[1]
    zn = min(CHIPS_Z, regs)
    n = groups * regs
    slots = 2 * n
    near, far = groups * zn, regs // zn
    lanes = segs * LANES
    board = [pltpu.VMEM((n, LANES), BF16)] * 12
    square = (width, width)
    operands = (
        anchors, directions, targets, region_ids.T, sample_counts.T,
        depth_index.transpose(1, 2, 0), frequencies, w_input, w_hidden, w_head[0].T,
    )
    shapes = (
        jax.ShapeDtypeStruct((3, rays), F32),
        jax.ShapeDtypeStruct(w_input.shape, BF16),
        jax.ShapeDtypeStruct(w_hidden.shape, BF16),
        jax.ShapeDtypeStruct((4, width), BF16),
    )
    scratch = [pltpu.VMEM(x.shape, x.dtype) for x in operands] + board + [
        pltpu.VMEM((n, LANES), F32),
        pltpu.VMEM((8, lanes), jnp.int32),
        pltpu.VMEM((32, lanes), F32),
        pltpu.VMEM((LANES, 2 * lanes), BF16),
        pltpu.VMEM((n, 2 * lanes), BF16),
        pltpu.VMEM((8, LANES), F32),
        pltpu.VMEM((8, width // 2), F32),
        pltpu.VMEM((32, slots), F32),
        pltpu.VMEM((width // 2, slots), F32),
        pltpu.VMEM((width // 2, slots), F32),
        pltpu.VMEM((samples, slots), F32),
        pltpu.VMEM((16, width), F32),
        pltpu.VMEM((4, samples, slots), F32),
        pltpu.VMEM((samples, 16, slots), F32),
        pltpu.VMEM((32, 2 * lanes), BF16),
        pltpu.VMEM(square, BF16),
        pltpu.VMEM(square, BF16),
        pltpu.VMEM(square, BF16),
        pltpu.VMEM(square, BF16),
        pltpu.VMEM(square, BF16),
        pltpu.VMEM((16, width), BF16),
        pltpu.VMEM((width, 16), BF16),
        pltpu.VMEM((samples, width, slots), BF16),
        pltpu.VMEM((3, samples, width, slots), BF16),
        pltpu.VMEM((3, samples, width, slots), BF16),
        pltpu.VMEM((3, samples, width, slots), BF16),
        pltpu.VMEM(square, F32),
        pltpu.VMEM(square, F32),
        pltpu.VMEM(square, F32),
        pltpu.VMEM((16, width), F32),
    ] + [pltpu.VMEM(x.shape, x.dtype) for x in shapes] + [
        pltpu.SemaphoreType.DMA((6,)),
        pltpu.SemaphoreType.DMA((6,)),
        pltpu.SemaphoreType.DMA((14,)),
    ]
    whole = pl.BlockSpec(memory_space=pltpu.HBM)
    made = pl.pallas_call(
        functools.partial(kernel, (groups, regs, zn, rays, segs, samples)),
        out_shape=shapes,
        in_specs=[whole] * 10,
        out_specs=[whole] * 4,
        scratch_shapes=scratch,
        compiler_params=pltpu.CompilerParams(
            collective_id=0, has_side_effects=True, vmem_limit_bytes=VMEM_BYTES
        ),
        name="radiance_step",
    )(*operands)
    colours, g_in, g_hid, g_head = pl.pallas_call(
        hand_over,
        out_shape=shapes,
        in_specs=[whole] * 4,
        out_specs=[whole] * 4,
        scratch_shapes=[pltpu.SemaphoreType.DMA((4,))],
        name="hand_over",
    )(*made)
    return colours, g_in, g_hid, g_head.T[None]


def solution(mesh):
    both = ("grp", "reg")
    return jax.shard_map(
        per_device,
        mesh=mesh,
        in_specs=(
            P(None, both), P(None, both), P(None, both), P(both, None), P(both, None),
            P(both, None, None), P(), P(both, None, None), P(both, None, None, None),
            P(both, None, None),
        ),
        out_specs=(
            P(None, both), P(both, None, None), P(both, None, None, None), P(both, None, None),
        ),
        check_vma=False,
    )
```

time: 73.1 us -> 63.8 us (0.87)
  local copies, waits for them, and re-layouts: 8.5 us -> 0 us
    pallas_call x1, Pallas kernels: 63.6 us -> 49.9 us  [per_device(): pl.pallas_call(functools.partial(kernel, (groups, regs, zn, rays, segs, s...]
    pallas_call x0 -> x1, Pallas kernels: none -> 13.2 us  [per_device(): pl.pallas_call(hand_over, out_shape=shapes, in_specs=[whole] * 4, out_spe...]
    unnamed x24 -> x0, local copies, waits for them, and re-layouts: 8.5 us -> none
where the time goes in v2:
time: 63.8 us; the launch traced here: 63.7 us
  Pallas kernels  63.1 us (99%)
  between operations  0.64 us (1%)
    pallas_call x1, Pallas kernels, per_device(): pl.pallas_call(functools.partial(kernel, (groups, regs, zn, rays, segs, s...  49.9 us
    pallas_call x1, Pallas kernels, per_device(): pl.pallas_call(hand_over, out_shape=shapes, in_specs=[whole] * 4, out_spe...  13.2 us

profile of v2, /device:TPU:1, one launch (start us, length us, event | category | flops | bytes accessed | tf_op | source)
XLA Modules:
  0.0 63.7 jit_solution(15209978566156786563)
XLA Ops:
  0.6 49.9 %radiance_step.1 = (f32[3,64]{1,0:T(4,128)}, bf16[1,256,256]{2,1,0:T(8,128)(2,1)}, bf16[1,2,256,256]{3,2,1,0:T(8,128)(2,1)}, bf16[4,256]{1,0:T(4,128)(2,1)}) custom-call(f32[3,64]{1,0:T(4,128)} %refs_0_.1, f32[3,64]{1,0:T(4,128)} %refs_1_.1, f32[3,64]{1,0:T(4,128)} %refs_2_.1, s32[4,64]{1,0:T(4,128)} %bitcast.10, s32[4,64]{1,0:T(4,128)} %bitcast.11, ...), custom_call_target="tpu_custom_call" | custom-call | tf_op jit(solution)/shard_map/radiance_step/pallas_call | solution.py:434
  50.5 13.2 %hand_over.1 = (f32[3,64]{1,0:T(4,128)}, bf16[1,256,256]{2,1,0:T(8,128)(2,1)}, bf16[1,2,256,256]{3,2,1,0:T(8,128)(2,1)}, bf16[4,256]{1,0:T(4,128)(2,1)}) custom-call(f32[3,64]{1,0:T(4,128)} %get-tuple-element.12.refs_0_, bf16[1,256,256]{2,1,0:T(8,128)(2,1)} %get-tuple-element.13.refs_1_, bf16[1,2,256,256]{3,2,1,0:T(8,128)(2,1)} %get-tuple-element.14.refs_2_, ...), custom_call_target="tpu_custom_call" | custom-call | tf_op jit(solution)/shard_map/hand_over/pallas_call | solution.py:445

commit v3 on v2

--- a/solution.py
+++ b/solution.py
@@ -72,6 +72,53 @@
     return everything.wait_recv, everything.wait_send
 
 
+def direct(source, target, row_of, own_row, slot, where, send, receive):
+    groups, side, zn, grp, me_y, me_x, me_z, regs = where
+
+    def ring(index):
+        half = index // 2 if isinstance(index, int) else lax.div(index, 2)
+        odd = index % 2 if isinstance(index, int) else lax.rem(index, 2)
+        return zn // 2 + half - odd * (2 * half + 1)
+
+    def layer(index, nearest):
+        z = lax.rem(me_z + ring(index), zn)
+        for y, x in sorted(
+            ((y, x) for y in range(side) for x in range(side)),
+            key=lambda q: -min(q[0], side - q[0]) - min(q[1], side - q[1]),
+        ):
+            far = lax.rem(me_y + y, side) * side + lax.rem(me_x + x, side)
+            for core in range(groups - 1, -1, -1):
+                if nearest and y == x == core == 0:
+                    continue
+                c = lax.rem(grp + core, groups)
+                pltpu.make_async_remote_copy(
+                    src_ref=source.at[pl.ds(row_of(c, far, z), 1)],
+                    dst_ref=target.at[pl.ds(own_row, 1)],
+                    send_sem=send,
+                    recv_sem=receive,
+                    device_id=(c, far * zn + z),
+                    device_id_type=MESH,
+                ).start()
+
+    def body(index, carry):
+        layer(index, False)
+        return carry
+
+    lax.fori_loop(0, zn - 1, body, 0)
+    layer(zn - 1, True)
+    target[pl.ds(own_row, 1), :] = source[pl.ds(slot, 1), :]
+    count = groups * regs - 1
+    everything = pltpu.make_async_remote_copy(
+        src_ref=source.at[pl.ds(0, count)],
+        dst_ref=target.at[pl.ds(0, count)],
+        send_sem=send,
+        recv_sem=receive,
+        device_id=(lax.rem(grp + 1, groups), (me_y * side + me_x) * zn + me_z),
+        device_id_type=MESH,
+    )
+    return everything.wait_recv, everything.wait_send
+
+
 def turned(source, loose, target, major, minor):
     loose[...] = source[...].astype(F32)
     for index in range(minor):
@@ -93,8 +140,7 @@
 ):
     arguments, results = refs[:10], refs[10:14]
     (
-    send1, mid1, turn1, last1, send2, mid2, turn2, last2, send3, mid3, turn3, last3,
-    loose, rows_s, words_s, words_b, onehot, target_s, freq_s, slots_s, phase0, phase1, depth_s, head_s,
+    send1, mid1, turn1, last1, loose, send2, last2, send3, last3, rows_s, words_s, words_b, onehot, freq_s, slots_s, phase0, phase1, depth_s, head_s,
     raw_s, graw_s, cot_b, w1t, w2t, w3t, w2, w3, wot, wo, encoded, hidden, slope, cotangents,
     acc1, acc2, acc3, acc4, colours, g_in, g_hid, g_head, sends, receives, local,
     ) = refs[24:]
@@ -111,7 +157,8 @@
     n = groups * regs
     near, far = groups * zn, regs // zn
     slots = 2 * n
-    width = segs * LANES
+    width = segs * rays
+    side = math.isqrt(far)
     features = wh.shape[-1]
     freqs = features // 2
 
@@ -127,6 +174,16 @@
     def far_device(index):
         return (grp, index * zn + me_z)
 
+    where = (groups, side, zn, grp, lax.div(me_far, side), lax.rem(me_far, side), me_z, regs)
+
+    def region_row(c, yx, z):
+        return (c * zn + z) * far + yx
+
+    def source_row(c, yx, z):
+        return yx * near + c * zn + z
+
+    my_region_row = region_row(grp, me_far, me_z)
+    my_source_row = source_row(grp, me_far, me_z)
     barrier = pltpu.get_barrier_semaphore()
 
     for count, me, device in ((near, me_near, near_device), (far, me_far, far_device)):
@@ -143,7 +200,7 @@
     rows_s[...] = jnp.full(rows_s.shape, -1, jnp.int32)
     words_s[...] = jnp.zeros(words_s.shape, F32)
     for k in range(segs):
-        part = slice(k * LANES, k * LANES + rays)
+        part = slice(k * rays, (k + 1) * rays)
         rows_s[0:1, part] = place[k : k + 1]
         both = jnp.concatenate([anchors[...], directions[...]], axis=0)
         high, middle, low = pieces(both)
@@ -191,12 +248,10 @@
     freq_s[...] = jnp.zeros(freq_s.shape, F32)
     freq_s[0:3, :] = frequencies[...] * (1.0 / (2.0 * math.pi))
     columns = freq_s[...].T
-    send2[...] = jnp.zeros(send2.shape, BF16)
-    send3[...] = jnp.zeros(send3.shape, BF16)
+    send2[...] = jnp.zeros(send2.shape, F32)
+    send3[...] = jnp.zeros(send3.shape, F32)
     graw_s[...] = jnp.zeros(graw_s.shape, F32)
     cot_b[...] = jnp.zeros(cot_b.shape, BF16)
-    target_s[...] = jnp.zeros(target_s.shape, F32)
-    target_s[0:3, 0:rays] = targets[...]
     wait_far1()
 
     words = last1[...].astype(F32).T
@@ -254,57 +309,47 @@
     blank = jnp.zeros((4, slots), F32)
     answer = jnp.concatenate(list(pieces(answer)) + [blank], axis=0)
     answer = jnp.concatenate([answer[:, 0:n], answer[:, n:]], axis=0)
-    send2[:, 0:32] = answer.T.astype(BF16)
-
-    wait_far2, sent_far2 = exchange(
-        send2, mid2, near, far, me_far, far_device, sends.at[2], receives.at[2]
+    send2[:, 0:32] = answer.T
+
+    wait2, sent2 = direct(
+        send2, last2, source_row, my_region_row, my_source_row, where, sends.at[2], receives.at[2]
     )
     d_density = 0.5 * live * clear * jnp.where(density >= 0.0, 1.0, small) / (1.0 + small)
     d_tone = [weight * t * (1.0 - t) for t in tone]
-    wait_far2()
-    turned(mid2, loose, turn2, far, near)
-    wait_near2, sent_near2 = exchange(
-        turn2, last2, far, near, me_near, near_device, sends.at[3], receives.at[3]
-    )
-    wait_near2()
-
-    values = last2[...].astype(F32).T[0:32].astype(BF16)
+    wait2()
+
+    values = last2[...].T[0:32].astype(BF16)
     found = dot(values[0:16], onehot[:, 0:width]) + dot(values[16:32], onehot[:, width:])
     found = (found[0:4] + found[4:8]) + found[8:12]
-    arrive = [jnp.ones((1, LANES), F32)]
-    total = jnp.zeros((3, LANES), F32)
+    arrive = [jnp.ones((1, rays), F32)]
+    total = jnp.zeros((3, rays), F32)
     parts = []
     for k in range(segs):
-        part = found[:, k * LANES : (k + 1) * LANES]
+        part = found[:, k * rays : (k + 1) * rays]
         parts.append(part)
         total = total + arrive[k] * part[0:3]
         arrive.append(arrive[k] * part[3:4])
     total = total + arrive[segs]
-    colours[...] = total[:, 0:rays]
-    error = total - target_s[0:3, :]
+    colours[...] = total
+    error = total - targets[...]
     behind = jnp.sum(error, axis=0, keepdims=True)
     for k in range(segs - 1, -1, -1):
         part = parts[k]
         cotangent = jnp.concatenate([arrive[k] * error, arrive[k] * behind], axis=0)
         behind = jnp.sum(error * part[0:3], axis=0, keepdims=True) + part[3:4] * behind
         stack = jnp.concatenate(
-            list(pieces(cotangent)) + [jnp.zeros((4, LANES), F32)], axis=0
+            list(pieces(cotangent)) + [jnp.zeros((4, rays), F32)], axis=0
         ).astype(BF16)
-        cot_b[0:16, k * LANES : (k + 1) * LANES] = stack
-        cot_b[16:32, width + k * LANES : width + (k + 1) * LANES] = stack
-    send3[:, 0:32] = dot_nt(onehot[...], cot_b[...]).astype(BF16)
-
-    wait_near3, sent_near3 = exchange(
-        send3, mid3, far, near, me_near, near_device, sends.at[4], receives.at[4]
-    )
-    wait_near3()
-    turned(mid3, loose, turn3, near, far)
-    wait_far3, sent_far3 = exchange(
-        turn3, last3, near, far, me_far, far_device, sends.at[5], receives.at[5]
-    )
-    wait_far3()
-
-    words = last3[...].astype(F32).T[0:32]
+        cot_b[0:16, k * rays : (k + 1) * rays] = stack
+        cot_b[16:32, width + k * rays : width + (k + 1) * rays] = stack
+    send3[:, 0:32] = dot_nt(onehot[...], cot_b[...])
+
+    wait3, sent3 = direct(
+        send3, last3, region_row, my_source_row, my_region_row, where, sends.at[3], receives.at[3]
+    )
+    wait3()
+
+    words = last3[...].T[0:32]
     given = jnp.concatenate(
         [(words[0:4] + words[4:8]) + words[8:12], (words[16:20] + words[20:24]) + words[24:28]],
         axis=1,
@@ -354,19 +399,26 @@
     for store in stores:
         store.wait()
 
-    for sent in (sent_near1, sent_far1, sent_far2, sent_near2, sent_near3, sent_far3):
+    for sent in (sent_near1, sent_far1, sent2, sent3):
         sent()
 
 
 def hand_over(*refs):
-    moves = [
-        pltpu.make_async_copy(refs[index], refs[4 + index], refs[8].at[index])
+    sources, results, places, sems = refs[:4], refs[4:8], refs[8:12], refs[12]
+    loads = [
+        pltpu.make_async_copy(sources[index], places[index], sems.at[index]) for index in range(4)
+    ]
+    stores = [
+        pltpu.make_async_copy(places[index], results[index], sems.at[4 + index])
         for index in range(4)
     ]
-    for move in moves:
-        move.start()
-    for move in moves:
-        move.wait()
+    for load in loads:
+        load.start()
+    for load, store in zip(loads, stores):
+        load.wait()
+        store.start()
+    for store in stores:
+        store.wait()
 
 
 def per_device(
@@ -381,8 +433,8 @@
     n = groups * regs
     slots = 2 * n
     near, far = groups * zn, regs // zn
-    lanes = segs * LANES
-    board = [pltpu.VMEM((n, LANES), BF16)] * 12
+    lanes = segs * rays
+    board = [pltpu.VMEM((n, LANES), BF16)] * 4 + [pltpu.VMEM((n, LANES), F32)] * 5
     square = (width, width)
     operands = (
         anchors, directions, targets, region_ids.T, sample_counts.T,
@@ -395,12 +447,10 @@
         jax.ShapeDtypeStruct((4, width), BF16),
     )
     scratch = [pltpu.VMEM(x.shape, x.dtype) for x in operands] + board + [
-        pltpu.VMEM((n, LANES), F32),
         pltpu.VMEM((8, lanes), jnp.int32),
         pltpu.VMEM((32, lanes), F32),
         pltpu.VMEM((LANES, 2 * lanes), BF16),
         pltpu.VMEM((n, 2 * lanes), BF16),
-        pltpu.VMEM((8, LANES), F32),
         pltpu.VMEM((8, width // 2), F32),
         pltpu.VMEM((32, slots), F32),
         pltpu.VMEM((width // 2, slots), F32),
@@ -426,8 +476,8 @@
         pltpu.VMEM(square, F32),
         pltpu.VMEM((16, width), F32),
     ] + [pltpu.VMEM(x.shape, x.dtype) for x in shapes] + [
-        pltpu.SemaphoreType.DMA((6,)),
-        pltpu.SemaphoreType.DMA((6,)),
+        pltpu.SemaphoreType.DMA((4,)),
+        pltpu.SemaphoreType.DMA((4,)),
         pltpu.SemaphoreType.DMA((14,)),
     ]
     whole = pl.BlockSpec(memory_space=pltpu.HBM)
@@ -447,7 +497,8 @@
         out_shape=shapes,
         in_specs=[whole] * 4,
         out_specs=[whole] * 4,
-        scratch_shapes=[pltpu.SemaphoreType.DMA((4,))],
+        scratch_shapes=[pltpu.VMEM(x.shape, x.dtype) for x in shapes]
+        + [pltpu.SemaphoreType.DMA((8,))],
         name="hand_over",
     )(*made)
     return colours, g_in, g_hid, g_head.T[None]

time: 63.8 us -> 49.9 us (0.78)
  Pallas kernels: 63.1 us -> 49 us
    pallas_call x1, Pallas kernels: 13.2 us -> 1.8 us  [per_device(): pl.pallas_call(hand_over, out_shape=shapes, in_specs=[whole] * 4, out_spe...]
    pallas_call x1, Pallas kernels: 49.9 us -> 47.2 us  [per_device(): pl.pallas_call(functools.partial(kernel, (groups, regs, zn, rays, segs, s...]
where the time goes in v3:
time: 49.9 us; the launch traced here: 49.8 us
  Pallas kernels  49 us (98%)
  between operations  0.8 us (2%)
    pallas_call x1, Pallas kernels, per_device(): pl.pallas_call(functools.partial(kernel, (groups, regs, zn, rays, segs, s...  47.2 us
    pallas_call x1, Pallas kernels, per_device(): pl.pallas_call(hand_over, out_shape=shapes, in_specs=[whole] * 4, out_spe...  1.8 us

profile of v3, /device:TPU:1, one launch (start us, length us, event | category | flops | bytes accessed | tf_op | source)
XLA Modules:
  0.0 49.8 jit_solution(4919911084462909251)
XLA Ops:
  0.6 47.2 %radiance_step.1 = (f32[3,64]{1,0:T(4,128)}, bf16[1,256,256]{2,1,0:T(8,128)(2,1)}, bf16[1,2,256,256]{3,2,1,0:T(8,128)(2,1)}, bf16[4,256]{1,0:T(4,128)(2,1)}) custom-call(f32[3,64]{1,0:T(4,128)} %refs_0_.1, f32[3,64]{1,0:T(4,128)} %refs_1_.1, f32[3,64]{1,0:T(4,128)} %refs_2_.1, s32[4,64]{1,0:T(4,128)} %bitcast.10, s32[4,64]{1,0:T(4,128)} %bitcast.11, ...), custom_call_target="tpu_custom_call" | custom-call | tf_op jit(solution)/shard_map/radiance_step/pallas_call | solution.py:484
  47.8 1.8 %hand_over.1 = (f32[3,64]{1,0:T(4,128)}, bf16[1,256,256]{2,1,0:T(8,128)(2,1)}, bf16[1,2,256,256]{3,2,1,0:T(8,128)(2,1)}, bf16[4,256]{1,0:T(4,128)(2,1)}) custom-call(f32[3,64]{1,0:T(4,128)} %get-tuple-element.12.refs_0_, bf16[1,256,256]{2,1,0:T(8,128)(2,1)} %get-tuple-element.13.refs_1_, bf16[1,2,256,256]{3,2,1,0:T(8,128)(2,1)} %get-tuple-element.14.refs_2_, ...), custom_call_target="tpu_custom_call" | custom-call | tf_op jit(solution)/shard_map/hand_over/pallas_call | solution.py:495

commit v4 on v3

--- a/solution.py
+++ b/solution.py
@@ -16,10 +16,10 @@
 F32 = jnp.float32
 BF16 = jnp.bfloat16
 
-SIN = (6.283182621002197, -41.34142303466797, 81.59620666503906, -76.58030700683594,
-       41.2061653137207, -12.272321701049805)
-COS = (1.0, -19.73920440673828, 64.93911743164062, -85.45016479492188, 60.16783142089844,
-       -25.968313217163086, 6.529609680175781)
+SIN = (4.442883014678955, -7.308241367340088, 3.6062893867492676, -0.8457654118537903,
+       0.10920875519514084)
+COS = (1.4142135381698608, -6.978850841522217, 5.7394609451293945, -1.8835630416870117,
+       0.31069818139076233)
 
 
 def horner(coefficients, x):
@@ -44,36 +44,104 @@
     return high, middle, (rest - middle).astype(BF16).astype(F32)
 
 
-def exchange(source, target, rows, count, me, device, send, receive):
-    def part(ref, index):
-        return ref.at[pl.ds(pl.multiple_of(index * rows, rows), rows)]
-
-    for step in range(1, count):
-        peer = lax.rem(me + step, count)
-        pltpu.make_async_remote_copy(
-            src_ref=part(source, peer),
-            dst_ref=part(target, me),
-            send_sem=send,
-            recv_sem=receive,
-            device_id=device(peer),
-            device_id_type=MESH,
-        ).start()
-    own = pl.ds(pl.multiple_of(me * rows, rows), rows)
-    target[own, :] = source[own, :]
-    others = pl.ds(0, (count - 1) * rows)
-    everything = pltpu.make_async_remote_copy(
-        src_ref=source.at[others],
-        dst_ref=target.at[others],
+def span(offset, size):
+    return min(offset, size - offset)
+
+
+def farthest_first(first, second):
+    offsets = [(a, b) for a in range(first) for b in range(second)]
+    return sorted(offsets, key=lambda q: (-span(q[0], first) - span(q[1], second), q))
+
+
+def ranks(side):
+    return {offset: place for place, offset in enumerate(reversed(farthest_first(side, side)))}
+
+
+class Place:
+    def __init__(self, groups, regs, zn):
+        self.groups, self.regs, self.zn = groups, regs, zn
+        self.side = math.isqrt(regs // zn)
+        self.grp = lax.axis_index("grp").astype(jnp.int32)
+        reg = lax.axis_index("reg").astype(jnp.int32)
+        self.z = lax.rem(reg, zn)
+        self.yx = lax.div(reg, zn)
+        self.y, self.x = lax.div(self.yx, self.side), lax.rem(self.yx, self.side)
+        self.near = self.grp * zn + self.z
+        self.rank = ranks(self.side)
+
+    def shifted(self, core=0, y=0, x=0, z=0):
+        c = lax.rem(self.grp + core, self.groups) if core else self.grp
+        line = lax.rem(self.y + y, self.side) if y else self.y
+        row = lax.rem(self.x + x, self.side) if x else self.x
+        layer = self.z if isinstance(z, int) and z == 0 else lax.rem(self.z + z, self.zn)
+        return c, line * self.side + row, layer
+
+    def device(self, peer):
+        return (peer[0], peer[1] * self.zn + peer[2])
+
+    def opposite(self, y, x):
+        return self.rank[(-y % self.side, -x % self.side)]
+
+    def near_offsets(self):
+        return [(c, z) for c, z in farthest_first(self.groups, self.zn) if (c, z) != (0, 0)]
+
+    def far_offsets(self):
+        return [(y, x) for y, x in farthest_first(self.side, self.side) if (y, x) != (0, 0)]
+
+
+def send_part(source, target, rows, start, end, send, receive, device):
+    part = pltpu.make_async_remote_copy(
+        src_ref=source.at[pl.ds(start, rows)],
+        dst_ref=target.at[pl.ds(end, rows)],
         send_sem=send,
         recv_sem=receive,
-        device_id=device(lax.rem(me + 1, count)),
+        device_id=device,
         device_id_type=MESH,
     )
-    return everything.wait_recv, everything.wait_send
-
-
-def direct(source, target, row_of, own_row, slot, where, send, receive):
-    groups, side, zn, grp, me_y, me_x, me_z, regs = where
+    part.start()
+
+
+def bytes_of(source, target, rows, send, receive, device):
+    return pltpu.make_async_remote_copy(
+        src_ref=source.at[pl.ds(0, rows)],
+        dst_ref=target.at[pl.ds(0, rows)],
+        send_sem=send,
+        recv_sem=receive,
+        device_id=device,
+        device_id_type=MESH,
+    )
+
+
+def near_exchange(at, source, target, rows, send, receive):
+    mine = pl.multiple_of(at.near * rows, rows)
+    for core, z in at.near_offsets():
+        peer = at.shifted(core=core, z=z)
+        start = pl.multiple_of((peer[0] * at.zn + peer[2]) * rows, rows)
+        send_part(source, target, rows, start, mine, send, receive, at.device(peer))
+    target[pl.ds(mine, rows), :] = source[pl.ds(mine, rows), :]
+    others = (at.groups * at.zn - 1) * rows
+    return bytes_of(source, target, others, send, receive, at.device(at.shifted(core=1)))
+
+
+def far_exchange(at, source, target, rows, send, receives):
+    count = at.side * at.side
+    for y, x in at.far_offsets():
+        peer = at.shifted(y=y, x=x)
+        start = pl.multiple_of(peer[1] * rows, rows)
+        end = at.opposite(y, x)
+        receive = receives.at[2 * end // count]
+        send_part(source, target, rows, start, end * rows, send, receive, at.device(peer))
+    target[0:rows, :] = source[pl.ds(pl.multiple_of(at.yx * rows, rows), rows), :]
+    device = at.device(at.shifted(y=1))
+    first, second = (count // 2 - 1) * rows, count // 2 * rows
+    return (
+        bytes_of(source, target, first, send, receives.at[0], device),
+        bytes_of(source, target, second, send, receives.at[1], device),
+    )
+
+
+def direct(at, source, target, start_of, end_of, send, receive):
+    zn = at.zn
 
     def ring(index):
         half = index // 2 if isinstance(index, int) else lax.div(index, 2)
@@ -81,24 +149,15 @@
         return zn // 2 + half - odd * (2 * half + 1)
 
     def layer(index, nearest):
-        z = lax.rem(me_z + ring(index), zn)
-        for y, x in sorted(
-            ((y, x) for y in range(side) for x in range(side)),
-            key=lambda q: -min(q[0], side - q[0]) - min(q[1], side - q[1]),
-        ):
-            far = lax.rem(me_y + y, side) * side + lax.rem(me_x + x, side)
-            for core in range(groups - 1, -1, -1):
+        for y, x in farthest_first(at.side, at.side):
+            for core in range(at.groups - 1, -1, -1):
                 if nearest and y == x == core == 0:
                     continue
-                c = lax.rem(grp + core, groups)
-                pltpu.make_async_remote_copy(
-                    src_ref=source.at[pl.ds(row_of(c, far, z), 1)],
-                    dst_ref=target.at[pl.ds(own_row, 1)],
-                    send_sem=send,
-                    recv_sem=receive,
-                    device_id=(c, far * zn + z),
-                    device_id_type=MESH,
-                ).start()
+                peer = at.shifted(core=core, y=y, x=x, z=0 if nearest else ring(index))
+                send_part(
+                    source, target, 1, start_of(peer, y, x), end_of(y, x), send, receive,
+                    at.device(peer),
+                )
 
     def body(index, carry):
         layer(index, False)
@@ -106,17 +165,10 @@
 
     lax.fori_loop(0, zn - 1, body, 0)
     layer(zn - 1, True)
-    target[pl.ds(own_row, 1), :] = source[pl.ds(slot, 1), :]
-    count = groups * regs - 1
-    everything = pltpu.make_async_remote_copy(
-        src_ref=source.at[pl.ds(0, count)],
-        dst_ref=target.at[pl.ds(0, count)],
-        send_sem=send,
-        recv_sem=receive,
-        device_id=(lax.rem(grp + 1, groups), (me_y * side + me_x) * zn + me_z),
-        device_id_type=MESH,
-    )
-    return everything.wait_recv, everything.wait_send
+    own = source[pl.ds(start_of(at.shifted(), 0, 0), 1), :]
+    target[pl.ds(end_of(0, 0), 1), :] = own
+    count = at.groups * at.regs - 1
+    return bytes_of(source, target, count, send, receive, at.device(at.shifted(core=1)))
 
 
 def turned(source, loose, target, major, minor):
@@ -158,39 +210,22 @@
     near, far = groups * zn, regs // zn
     slots = 2 * n
     width = segs * rays
-    side = math.isqrt(far)
     features = wh.shape[-1]
     freqs = features // 2
 
-    grp = lax.axis_index("grp").astype(jnp.int32)
-    reg = lax.axis_index("reg").astype(jnp.int32)
-    me_far = lax.div(reg, zn)
-    me_z = lax.rem(reg, zn)
-    me_near = grp * zn + me_z
-
-    def near_device(index):
-        return (lax.div(index, zn), me_far * zn + lax.rem(index, zn))
-
-    def far_device(index):
-        return (grp, index * zn + me_z)
-
-    where = (groups, side, zn, grp, lax.div(me_far, side), lax.rem(me_far, side), me_z, regs)
-
-    def region_row(c, yx, z):
-        return (c * zn + z) * far + yx
-
-    def source_row(c, yx, z):
-        return yx * near + c * zn + z
-
-    my_region_row = region_row(grp, me_far, me_z)
-    my_source_row = source_row(grp, me_far, me_z)
+    at = Place(groups, regs, zn)
+
+    def region_row(peer, y=0, x=0):
+        return (peer[0] * zn + peer[2]) * far + peer[1]
+
+    def source_row(peer, y, x):
+        return at.rank[(y, x)] * near + peer[0] * zn + peer[2]
+
     barrier = pltpu.get_barrier_semaphore()
-
-    for count, me, device in ((near, me_near, near_device), (far, me_far, far_device)):
-        for step in range(1, count):
-            pl.semaphore_signal(
-                barrier, inc=1, device_id=device(lax.rem(me + step, count)), device_id_type=MESH
-            )
+    greeted = [at.shifted(core=c, z=z) for c, z in at.near_offsets()]
+    greeted += [at.shifted(y=y, x=x) for y, x in at.far_offsets()]
+    for peer in greeted:
+        pl.semaphore_signal(barrier, inc=1, device_id=at.device(peer), device_id_type=MESH)
     for index in (0, 1, 3, 4, 5):
         loads[index].wait()
 
@@ -224,9 +259,7 @@
 
     pl.semaphore_wait(barrier, near + far - 2)
 
-    wait_near1, sent_near1 = exchange(
-        send1, mid1, far, near, me_near, near_device, sends.at[0], receives.at[0]
-    )
+    near1 = near_exchange(at, send1, mid1, far, sends.at[0], receives.at[0])
     for index in (2, 6, 7, 8, 9):
         loads[index].wait()
     w1t[...] = (w1[0].astype(F32) * 0.5).T.astype(BF16)
@@ -236,11 +269,9 @@
     half3 = wh[0, 1].astype(F32) * 0.5
     w3[...] = half3.astype(BF16)
     w3t[...] = half3.T.astype(BF16)
-    wait_near1()
+    near1.wait_recv()
     turned(mid1, loose, turn1, near, far)
-    wait_far1, sent_far1 = exchange(
-        turn1, last1, near, far, me_far, far_device, sends.at[1], receives.at[1]
-    )
+    halves = far_exchange(at, turn1, last1, near, sends.at[1], receives.at[pl.ds(1, 2)])
     head_s[...] = jnp.zeros(head_s.shape, F32)
     head_s[0:4, :] = w_head[...].astype(F32)
     wot[...] = head_s[...].astype(BF16)
@@ -252,44 +283,60 @@
     send3[...] = jnp.zeros(send3.shape, F32)
     graw_s[...] = jnp.zeros(graw_s.shape, F32)
     cot_b[...] = jnp.zeros(cot_b.shape, BF16)
-    wait_far1()
-
-    words = last1[...].astype(F32).T
-    slots_s[:, 0:n] = words[0:32]
-    slots_s[:, n:] = words[32:64]
-    geometry = (slots_s[0:6, :] + slots_s[6:12, :]) + slots_s[12:18, :]
-    base = jnp.zeros((freqs, slots), F32)
-    rate = jnp.zeros((freqs, slots), F32)
-    for c in range(3):
-        base = base + columns[:, c : c + 1] * geometry[c : c + 1]
-        rate = rate + columns[:, c : c + 1] * geometry[3 + c : 4 + c]
-    phase0[...] = base
-    phase1[...] = rate
-    depth_s[...] = 0.1 + (slots_s[24 : 24 + samples, :] + 0.5) * (2.0 / DEPTHS)
+
+    lane = n // 2
+    part = 2 * lane
+
+    def decode(half):
+        words = last1[half * lane : (half + 1) * lane, :].astype(F32).T
+        there = slice(half * part, (half + 1) * part)
+        slots_s[:, half * part : half * part + lane] = words[0:32]
+        slots_s[:, half * part + lane : (half + 1) * part] = words[32:64]
+        geometry = (slots_s[0:6, there] + slots_s[6:12, there]) + slots_s[12:18, there]
+        base = jnp.zeros((freqs, part), F32)
+        rate = jnp.zeros((freqs, part), F32)
+        for c in range(3):
+            base = base + columns[:, c : c + 1] * geometry[c : c + 1]
+            rate = rate + columns[:, c : c + 1] * geometry[3 + c : 4 + c]
+        phase0[:, there] = base
+        phase1[:, there] = rate
+        depth_s[:, there] = 0.1 + (slots_s[24 : 24 + samples, there] + 0.5) * (2.0 / DEPTHS)
+
+    layers = (w1t, w2t, w3t)
+    for stage, item in staged(5, samples):
+        half, first = divmod(2 * item, samples)
+        there = slice(half * part, (half + 1) * part)
+        if stage == 0:
+            if first == 0:
+                halves[half].wait_recv()
+                decode(half)
+            for side in range(2):
+                turns = phase0[:, there] + depth_s[first + side : first + side + 1, there] * phase1[:, there]
+                r = turns - jnp.round(turns)
+                square = r * r
+                sine = r * horner(SIN, square)
+                columns_of = slice(side * part, (side + 1) * part)
+                encoded[item, 0:freqs, columns_of] = (sine * horner(COS, square)).astype(BF16)
+                encoded[item, freqs:, columns_of] = (1.0 - sine * sine).astype(BF16)
+        elif stage < 4:
+            z = dot(
+                layers[stage - 1][...], encoded[item] if stage == 1 else hidden[stage - 2, item]
+            )
+            t = jnp.tanh(z)
+            hidden[stage - 1, item] = (z + z * t).astype(BF16)
+            slope[stage - 1, item] = t.astype(BF16)
+        else:
+            raw = dot(wot[...], hidden[2, item])
+            for side in range(2):
+                for k in range(4):
+                    raw_s[k, first + side : first + side + 1, there] = raw[
+                        k : k + 1, side * part : (side + 1) * part
+                    ]
+
     live = jnp.where(
         lax.broadcasted_iota(jnp.int32, (samples, slots), 0).astype(F32) < slots_s[18:19, :],
         1.0, 0.0,
     )
-
-    layers = (w1t, w2t, w3t)
-    for stage, j in staged(5, samples):
-        if stage == 0:
-            turns = phase0[...] + depth_s[j : j + 1, :] * phase1[...]
-            r = turns - jnp.round(turns)
-            square = r * r
-            encoded[j, 0:freqs] = (r * horner(SIN, square)).astype(BF16)
-            encoded[j, freqs:] = horner(COS, square).astype(BF16)
-        elif stage < 4:
-            z = dot(layers[stage - 1][...], encoded[j] if stage == 1 else hidden[stage - 2, j])
-            t = jnp.tanh(z)
-            h = z + z * t
-            hidden[stage - 1, j] = h.astype(BF16)
-            slope[stage - 1, j] = ((1.0 + h) + t * (1.0 - h)).astype(BF16)
-        else:
-            raw = dot(wot[...], hidden[2, j])
-            for k in range(4):
-                raw_s[k, j : j + 1, :] = raw[k : k + 1]
-
     density = raw_s[0]
     small = jnp.exp(-jnp.abs(density))
     softplus = jnp.maximum(density, 0.0) + jnp.log1p(small)
@@ -308,15 +355,31 @@
     answer = jnp.concatenate(seg, axis=0)
     blank = jnp.zeros((4, slots), F32)
     answer = jnp.concatenate(list(pieces(answer)) + [blank], axis=0)
-    answer = jnp.concatenate([answer[:, 0:n], answer[:, n:]], axis=0)
+    answer = jnp.concatenate(
+        [
+            jnp.concatenate([answer[:, 0:lane], answer[:, part : part + lane]], axis=1),
+            jnp.concatenate([answer[:, lane:part], answer[:, part + lane :]], axis=1),
+        ],
+        axis=0,
+    )
     send2[:, 0:32] = answer.T
 
-    wait2, sent2 = direct(
-        send2, last2, source_row, my_region_row, my_source_row, where, sends.at[2], receives.at[2]
-    )
+    back = direct(
+        at, send2, last2, source_row, lambda y, x: region_row(at.shifted()), sends.at[2],
+        receives.at[3],
+    )
+
+    def slopes(item, carry):
+        for index in range(3):
+            h = hidden[index, item].astype(F32)
+            t = slope[index, item].astype(F32)
+            slope[index, item] = ((1.0 + h) + t * (1.0 - h)).astype(BF16)
+        return carry
+
+    lax.fori_loop(0, samples, slopes, 0)
     d_density = 0.5 * live * clear * jnp.where(density >= 0.0, 1.0, small) / (1.0 + small)
     d_tone = [weight * t * (1.0 - t) for t in tone]
-    wait2()
+    back.wait_recv()
 
     values = last2[...].T[0:32].astype(BF16)
     found = dot(values[0:16], onehot[:, 0:width]) + dot(values[16:32], onehot[:, width:])
@@ -325,18 +388,18 @@
     total = jnp.zeros((3, rays), F32)
     parts = []
     for k in range(segs):
-        part = found[:, k * rays : (k + 1) * rays]
-        parts.append(part)
-        total = total + arrive[k] * part[0:3]
-        arrive.append(arrive[k] * part[3:4])
+        found_part = found[:, k * rays : (k + 1) * rays]
+        parts.append(found_part)
+        total = total + arrive[k] * found_part[0:3]
+        arrive.append(arrive[k] * found_part[3:4])
     total = total + arrive[segs]
     colours[...] = total
     error = total - targets[...]
     behind = jnp.sum(error, axis=0, keepdims=True)
     for k in range(segs - 1, -1, -1):
-        part = parts[k]
+        found_part = parts[k]
         cotangent = jnp.concatenate([arrive[k] * error, arrive[k] * behind], axis=0)
-        behind = jnp.sum(error * part[0:3], axis=0, keepdims=True) + part[3:4] * behind
+        behind = jnp.sum(error * found_part[0:3], axis=0, keepdims=True) + found_part[3:4] * behind
         stack = jnp.concatenate(
             list(pieces(cotangent)) + [jnp.zeros((4, rays), F32)], axis=0
         ).astype(BF16)
@@ -344,15 +407,18 @@
         cot_b[16:32, width + k * rays : width + (k + 1) * rays] = stack
     send3[:, 0:32] = dot_nt(onehot[...], cot_b[...])
 
-    wait3, sent3 = direct(
-        send3, last3, region_row, my_source_row, my_region_row, where, sends.at[3], receives.at[3]
-    )
-    wait3()
+    forth = direct(
+        at, send3, last3, region_row, lambda y, x: at.opposite(y, x) * near + at.near,
+        sends.at[3], receives.at[4],
+    )
+    forth.wait_recv()
 
     words = last3[...].T[0:32]
+    given = [
+        (words[q : q + 4] + words[q + 4 : q + 8]) + words[q + 8 : q + 12] for q in (0, 16)
+    ]
     given = jnp.concatenate(
-        [(words[0:4] + words[4:8]) + words[8:12], (words[16:20] + words[20:24]) + words[24:28]],
-        axis=1,
+        [given[0][:, 0:lane], given[1][:, 0:lane], given[0][:, lane:], given[1][:, lane:]], axis=1
     )
     gain = given[0:1] * tone[0] + given[1:2] * tone[1] + given[2:3] * tone[2]
     after = given[3:4]
@@ -362,10 +428,19 @@
         after = alpha[i : i + 1] * gain[i : i + 1] + keep[i : i + 1] * after
     d_raw = [jnp.concatenate(backs[::-1], axis=0) * d_density]
     d_raw += [given[c : c + 1] * d_tone[c] for c in range(3)]
-    for j in range(samples):
-        for k in range(4):
-            graw_s[j, k : k + 1, :] = d_raw[k][j : j + 1]
-
+    for item in range(samples):
+        half, first = divmod(2 * item, samples)
+        for side in range(2):
+            for k in range(4):
+                graw_s[item, k : k + 1, side * part : (side + 1) * part] = d_raw[k][
+                    first + side : first + side + 1, half * part : (half + 1) * part
+                ]
+
+    stores = [
+        pltpu.make_async_copy(place, result, local.at[10 + index])
+        for index, (place, result) in enumerate(zip(made, results))
+    ]
+    stores[0].start()
     backs = (wo, w3, w2)
     inputs = (lambda j: hidden[1, j], lambda j: hidden[0, j], lambda j: encoded[j])
     totals = (acc3, acc2, acc1)
@@ -376,6 +451,12 @@
         else:
             total[...] += term
 
+    ends = (
+        (3, g_head, lambda: acc4[0:4, :]),
+        (2, g_hid.at[0, 1], lambda: acc3[...]),
+        (2, g_hid.at[0, 0], lambda: acc2[...]),
+        (1, g_in.at[0], lambda: acc1[...]),
+    )
     for stage, j in staged(4, samples):
         if stage == 0:
             gather(acc4, j, dot_nt(graw_s[j].astype(BF16), hidden[2, j]))
@@ -385,22 +466,16 @@
             cotangents[stage, j] = g.astype(BF16)
         if stage > 0:
             gather(totals[stage - 1], j, dot_nt(inputs[stage - 1](j), cotangents[stage - 1, j]))
-
-    g_in[0] = acc1[...].astype(BF16)
-    g_hid[0, 0] = acc2[...].astype(BF16)
-    g_hid[0, 1] = acc3[...].astype(BF16)
-    g_head[...] = acc4[0:4, :].astype(BF16)
-    stores = [
-        pltpu.make_async_copy(place, result, local.at[10 + index])
-        for index, (place, result) in enumerate(zip(made, results))
-    ]
-    for store in stores:
-        store.start()
+        if j == samples - 1:
+            index, place, value = ends[stage]
+            place[...] = value().astype(BF16)
+            if stage != 1:
+                stores[index].start()
+
+    for sent in (near1, *halves, back, forth):
+        sent.wait_send()
     for store in stores:
         store.wait()
-
-    for sent in (sent_near1, sent_far1, sent2, sent3):
-        sent()
 
 
 def hand_over(*refs):
@@ -477,7 +552,7 @@
         pltpu.VMEM((16, width), F32),
     ] + [pltpu.VMEM(x.shape, x.dtype) for x in shapes] + [
         pltpu.SemaphoreType.DMA((4,)),
-        pltpu.SemaphoreType.DMA((4,)),
+        pltpu.SemaphoreType.DMA((5,)),
         pltpu.SemaphoreType.DMA((14,)),
     ]
     whole = pl.BlockSpec(memory_space=pltpu.HBM)

time: 49.9 us -> 47.1 us (0.944)
  Pallas kernels: 49 us -> 46.3 us
    pallas_call x1, Pallas kernels: 47.2 us -> 44.5 us  [per_device(): pl.pallas_call(functools.partial(kernel, (groups, regs, zn, rays, segs, s...]
where the time goes in v4:
time: 47.1 us; the launch traced here: 46.9 us
  Pallas kernels  46.3 us (98%)
  between operations  0.64 us (1%)
    pallas_call x1, Pallas kernels, per_device(): pl.pallas_call(functools.partial(kernel, (groups, regs, zn, rays, segs, s...  44.5 us
    pallas_call x1, Pallas kernels, per_device(): pl.pallas_call(hand_over, out_shape=shapes, in_specs=[whole] * 4, out_spe...  1.8 us

profile of v4, /device:TPU:1, one launch (start us, length us, event | category | flops | bytes accessed | tf_op | source)
XLA Modules:
  0.0 46.9 jit_solution(16980348495750185770)
XLA Ops:
  0.6 44.5 %radiance_step.1 = (f32[3,64]{1,0:T(4,128)}, bf16[1,256,256]{2,1,0:T(8,128)(2,1)}, bf16[1,2,256,256]{3,2,1,0:T(8,128)(2,1)}, bf16[4,256]{1,0:T(4,128)(2,1)}) custom-call(f32[3,64]{1,0:T(4,128)} %refs_0_.1, f32[3,64]{1,0:T(4,128)} %refs_1_.1, f32[3,64]{1,0:T(4,128)} %refs_2_.1, s32[4,64]{1,0:T(4,128)} %bitcast.10, s32[4,64]{1,0:T(4,128)} %bitcast.11, ...), custom_call_target="tpu_custom_call" | custom-call | tf_op jit(solution)/shard_map/radiance_step/pallas_call | solution.py:559
  45.1 1.8 %hand_over.1 = (f32[3,64]{1,0:T(4,128)}, bf16[1,256,256]{2,1,0:T(8,128)(2,1)}, bf16[1,2,256,256]{3,2,1,0:T(8,128)(2,1)}, bf16[4,256]{1,0:T(4,128)(2,1)}) custom-call(f32[3,64]{1,0:T(4,128)} %get-tuple-element.12.refs_0_, bf16[1,256,256]{2,1,0:T(8,128)(2,1)} %get-tuple-element.13.refs_1_, bf16[1,2,256,256]{3,2,1,0:T(8,128)(2,1)} %get-tuple-element.14.refs_2_, ...), custom_call_target="tpu_custom_call" | custom-call | tf_op jit(solution)/shard_map/hand_over/pallas_call | solution.py:570

commit v5 on v4

--- a/solution.py
+++ b/solution.py
@@ -69,12 +69,18 @@
         self.near = self.grp * zn + self.z
         self.rank = ranks(self.side)
 
+        def turns(mine, size):
+            return [mine] + [lax.rem(mine + step, size) for step in range(1, size)]
+
+        self.cores = turns(self.grp, groups)
+        self.layers = turns(self.z, zn)
+        ys, xs = turns(self.y, self.side), turns(self.x, self.side)
+        self.lines = {
+            (y, x): ys[y] * self.side + xs[x] for y in range(self.side) for x in range(self.side)
+        }
+
     def shifted(self, core=0, y=0, x=0, z=0):
-        c = lax.rem(self.grp + core, self.groups) if core else self.grp
-        line = lax.rem(self.y + y, self.side) if y else self.y
-        row = lax.rem(self.x + x, self.side) if x else self.x
-        layer = self.z if isinstance(z, int) and z == 0 else lax.rem(self.z + z, self.zn)
-        return c, line * self.side + row, layer
+        return self.cores[core], self.lines[(y, x)], self.layers[z]
 
     def device(self, peer):
         return (peer[0], peer[1] * self.zn + peer[2])
@@ -140,33 +146,34 @@
     )
 
 
-def direct(at, source, target, start_of, end_of, send, receive):
-    zn = at.zn
-
-    def ring(index):
-        half = index // 2 if isinstance(index, int) else lax.div(index, 2)
-        odd = index % 2 if isinstance(index, int) else lax.rem(index, 2)
-        return zn // 2 + half - odd * (2 * half + 1)
-
-    def layer(index, nearest):
-        for y, x in farthest_first(at.side, at.side):
+def direct(at, source, target, start, end_of, send, receive):
+    zn, lines = at.zn, farthest_first(at.side, at.side)
+    devices = {offset: at.lines[offset] * zn for offset in lines}
+    starts = {offset: start[2](*offset) for offset in lines}
+    ends = {offset: end_of(*offset) for offset in lines}
+    of_core = [core * start[0] for core in at.cores]
+
+    def layer(z, nearest):
+        bases = [base + z * start[1] for base in of_core]
+        for offset in lines:
             for core in range(at.groups - 1, -1, -1):
-                if nearest and y == x == core == 0:
+                if nearest and offset == (0, 0) and core == 0:
                     continue
-                peer = at.shifted(core=core, y=y, x=x, z=0 if nearest else ring(index))
                 send_part(
-                    source, target, 1, start_of(peer, y, x), end_of(y, x), send, receive,
-                    at.device(peer),
+                    source, target, 1, bases[core] + starts[offset], ends[offset], send, receive,
+                    (at.cores[core], devices[offset] + z),
                 )
 
     def body(index, carry):
-        layer(index, False)
+        half, odd = lax.div(index, 2), lax.rem(index, 2)
+        ring = zn // 2 + half - odd * (2 * half + 1)
+        layer(lax.rem(at.z + ring, zn), False)
         return carry
 
     lax.fori_loop(0, zn - 1, body, 0)
-    layer(zn - 1, True)
-    own = source[pl.ds(start_of(at.shifted(), 0, 0), 1), :]
-    target[pl.ds(end_of(0, 0), 1), :] = own
+    layer(at.z, True)
+    own = of_core[0] + at.z * start[1] + starts[(0, 0)]
+    target[pl.ds(ends[(0, 0)], 1), :] = source[pl.ds(own, 1), :]
     count = at.groups * at.regs - 1
     return bytes_of(source, target, count, send, receive, at.device(at.shifted(core=1)))
 
@@ -215,12 +222,9 @@
 
     at = Place(groups, regs, zn)
 
-    def region_row(peer, y=0, x=0):
-        return (peer[0] * zn + peer[2]) * far + peer[1]
-
-    def source_row(peer, y, x):
-        return at.rank[(y, x)] * near + peer[0] * zn + peer[2]
-
+    region_row = (zn * far, far, lambda y, x: at.lines[(y, x)])
+    source_row = (zn, 1, lambda y, x: at.rank[(y, x)] * near)
+    my_region_row = at.near * far + at.yx
     barrier = pltpu.get_barrier_semaphore()
     greeted = [at.shifted(core=c, z=z) for c, z in at.near_offsets()]
     greeted += [at.shifted(y=y, x=x) for y, x in at.far_offsets()]
@@ -365,8 +369,7 @@
     send2[:, 0:32] = answer.T
 
     back = direct(
-        at, send2, last2, source_row, lambda y, x: region_row(at.shifted()), sends.at[2],
-        receives.at[3],
+        at, send2, last2, source_row, lambda y, x: my_region_row, sends.at[2], receives.at[3]
     )
 
     def slopes(item, carry):
@@ -480,19 +483,28 @@
 
 def hand_over(*refs):
     sources, results, places, sems = refs[:4], refs[4:8], refs[8:12], refs[12]
-    loads = [
-        pltpu.make_async_copy(sources[index], places[index], sems.at[index]) for index in range(4)
+    width = sources[1].shape[1]
+    half = width // 2
+    pieces_of = [(0, ()), (3, ())]
+    pieces_of += [(2, (0, k, pl.ds(h, half))) for k in range(2) for h in (0, half)]
+    pieces_of += [(1, (0, pl.ds(h, half))) for h in (0, half)]
+
+    def part(group, index, where):
+        return group[index].at[where] if where else group[index]
+
+    moves = [
+        tuple(
+            pltpu.make_async_copy(part(a, index, where), part(b, index, where), sems.at[row, number])
+            for row, (a, b) in enumerate(((sources, places), (places, results)))
+        )
+        for number, (index, where) in enumerate(pieces_of)
     ]
-    stores = [
-        pltpu.make_async_copy(places[index], results[index], sems.at[4 + index])
-        for index in range(4)
-    ]
-    for load in loads:
+    for load, _ in moves:
         load.start()
-    for load, store in zip(loads, stores):
+    for load, store in moves:
         load.wait()
         store.start()
-    for store in stores:
+    for _, store in moves:
         store.wait()
 
 
@@ -573,7 +585,7 @@
         in_specs=[whole] * 4,
         out_specs=[whole] * 4,
         scratch_shapes=[pltpu.VMEM(x.shape, x.dtype) for x in shapes]
-        + [pltpu.SemaphoreType.DMA((8,))],
+        + [pltpu.SemaphoreType.DMA((2, 8))],
         name="hand_over",
     )(*made)
     return colours, g_in, g_hid, g_head.T[None]

time: 47.1 us -> 47.1 us (level)
  no operation moved by 1% of the time
where the time goes in v5:
time: 47.1 us; the launch traced here: 46.9 us
  Pallas kernels  46.3 us (98%)
  between operations  0.64 us (1%)
    pallas_call x1, Pallas kernels, per_device(): pl.pallas_call(functools.partial(kernel, (groups, regs, zn, rays, segs, s...  44.5 us
    pallas_call x1, Pallas kernels, per_device(): pl.pallas_call(hand_over, out_shape=shapes, in_specs=[whole] * 4, out_spe...  1.78 us

profile of v5, /device:TPU:1, one launch (start us, length us, event | category | flops | bytes accessed | tf_op | source)
XLA Modules:
  0.0 46.9 jit_solution(1270588590661351378)
XLA Ops:
  0.6 44.5 %radiance_step.1 = (f32[3,64]{1,0:T(4,128)}, bf16[1,256,256]{2,1,0:T(8,128)(2,1)}, bf16[1,2,256,256]{3,2,1,0:T(8,128)(2,1)}, bf16[4,256]{1,0:T(4,128)(2,1)}) custom-call(f32[3,64]{1,0:T(4,128)} %refs_0_.1, f32[3,64]{1,0:T(4,128)} %refs_1_.1, f32[3,64]{1,0:T(4,128)} %refs_2_.1, s32[4,64]{1,0:T(4,128)} %bitcast.10, s32[4,64]{1,0:T(4,128)} %bitcast.11, ...), custom_call_target="tpu_custom_call" | custom-call | tf_op jit(solution)/shard_map/radiance_step/pallas_call | solution.py:571
  45.1 1.8 %hand_over.1 = (f32[3,64]{1,0:T(4,128)}, bf16[1,256,256]{2,1,0:T(8,128)(2,1)}, bf16[1,2,256,256]{3,2,1,0:T(8,128)(2,1)}, bf16[4,256]{1,0:T(4,128)(2,1)}) custom-call(f32[3,64]{1,0:T(4,128)} %get-tuple-element.12.refs_0_, bf16[1,256,256]{2,1,0:T(8,128)(2,1)} %get-tuple-element.13.refs_1_, bf16[1,2,256,256]{3,2,1,0:T(8,128)(2,1)} %get-tuple-element.14.refs_2_, ...), custom_call_target="tpu_custom_call" | custom-call | tf_op jit(solution)/shard_map/hand_over/pallas_call | solution.py:582

commit v6 on v4

--- a/solution.py
+++ b/solution.py
@@ -179,6 +179,12 @@
         ].astype(BF16)
 
 
+def picks(count, shape):
+    row = lax.broadcasted_iota(jnp.int32, shape, 0)
+    lane = lax.broadcasted_iota(jnp.int32, shape, 1)
+    return jnp.where(count(row, lane), 1.0, 0.0).astype(BF16)
+
+
 def staged(stages, count):
     for step in range(count + stages - 1):
         for stage in range(stages):
@@ -192,7 +198,7 @@
 ):
     arguments, results = refs[:10], refs[10:14]
     (
-    send1, mid1, turn1, last1, loose, send2, last2, send3, last3, rows_s, words_s, words_b, onehot, freq_s, slots_s, phase0, phase1, depth_s, head_s,
+    send1, mid1, turn1, last1, loose, send2, last2, send3, last3, rows_s, words_s, words_b, onehot, freq_s, count_s, pick_s, phase0, phase1, depth_s, head_s,
     raw_s, graw_s, cot_b, w1t, w2t, w3t, w2, w3, wot, wo, encoded, hidden, slope, cotangents,
     acc1, acc2, acc3, acc4, colours, g_in, g_hid, g_head, sends, receives, local,
     ) = refs[24:]
@@ -204,8 +210,6 @@
         pltpu.make_async_copy(argument, place, local.at[index])
         for index, (argument, place) in enumerate(zip(arguments, held))
     ]
-    for load in loads:
-        load.start()
     n = groups * regs
     near, far = groups * zn, regs // zn
     slots = 2 * n
@@ -226,6 +230,8 @@
     greeted += [at.shifted(y=y, x=x) for y, x in at.far_offsets()]
     for peer in greeted:
         pl.semaphore_signal(barrier, inc=1, device_id=at.device(peer), device_id_type=MESH)
+    for load in loads:
+        load.start()
     for index in (0, 1, 3, 4, 5):
         loads[index].wait()
 
@@ -269,6 +275,19 @@
     half3 = wh[0, 1].astype(F32) * 0.5
     w3[...] = half3.astype(BF16)
     w3t[...] = half3.T.astype(BF16)
+    def first_words(row, lane):
+        word, q, place = row & 15, row >> 4, lane - (row >> 4) * 32
+        geometry = (word < 6) & ((place == word) | (place == word + 6) | (place == word + 12))
+        single = ((word == 6) & (place == 18)) | ((word >= 8) & (place == word + 16))
+        return (q < 2) & (place >= 0) & (place < 32) & (geometry | single)
+
+    pick_s[0:32, :] = picks(first_words, (32, LANES))
+    pick_s[32:64, :] = picks(lambda row, lane: row == lane, (32, LANES))
+    pick_s[64:80, :] = picks(
+        lambda row, lane: (row < 8) & (lane < 32) & (lane >> 4 == row >> 2)
+        & (lane & 3 == row & 3) & (lane & 15 < 12),
+        (16, LANES),
+    )
     near1.wait_recv()
     turned(mid1, loose, turn1, near, far)
     halves = far_exchange(at, turn1, last1, near, sends.at[1], receives.at[pl.ds(1, 2)])
@@ -288,11 +307,10 @@
     part = 2 * lane
 
     def decode(half):
-        words = last1[half * lane : (half + 1) * lane, :].astype(F32).T
+        words = dot_nt(pick_s[0:32, :], last1[half * lane : (half + 1) * lane, :])
         there = slice(half * part, (half + 1) * part)
-        slots_s[:, half * part : half * part + lane] = words[0:32]
-        slots_s[:, half * part + lane : (half + 1) * part] = words[32:64]
-        geometry = (slots_s[0:6, there] + slots_s[6:12, there]) + slots_s[12:18, there]
+        geometry = jnp.concatenate([words[0:8], words[16:24]], axis=1)
+        count_s[:, there] = geometry
         base = jnp.zeros((freqs, part), F32)
         rate = jnp.zeros((freqs, part), F32)
         for c in range(3):
@@ -300,7 +318,8 @@
             rate = rate + columns[:, c : c + 1] * geometry[3 + c : 4 + c]
         phase0[:, there] = base
         phase1[:, there] = rate
-        depth_s[:, there] = 0.1 + (slots_s[24 : 24 + samples, there] + 0.5) * (2.0 / DEPTHS)
+        index = jnp.concatenate([words[8 : 8 + samples], words[24 : 24 + samples]], axis=1)
+        depth_s[:, there] = 0.1 + (index + 0.5) * (2.0 / DEPTHS)
 
     layers = (w1t, w2t, w3t)
     for stage, item in staged(5, samples):
@@ -334,7 +353,7 @@
                     ]
 
     live = jnp.where(
-        lax.broadcasted_iota(jnp.int32, (samples, slots), 0).astype(F32) < slots_s[18:19, :],
+        lax.broadcasted_iota(jnp.int32, (samples, slots), 0).astype(F32) < count_s[6:7, :],
         1.0, 0.0,
     )
     density = raw_s[0]
@@ -381,7 +400,7 @@
     d_tone = [weight * t * (1.0 - t) for t in tone]
     back.wait_recv()
 
-    values = last2[...].T[0:32].astype(BF16)
+    values = dot_nt(pick_s[32:64, :], last2[...].astype(BF16)).astype(BF16)
     found = dot(values[0:16], onehot[:, 0:width]) + dot(values[16:32], onehot[:, width:])
     found = (found[0:4] + found[4:8]) + found[8:12]
     arrive = [jnp.ones((1, rays), F32)]
@@ -413,12 +432,9 @@
     )
     forth.wait_recv()
 
-    words = last3[...].T[0:32]
-    given = [
-        (words[q : q + 4] + words[q + 4 : q + 8]) + words[q + 8 : q + 12] for q in (0, 16)
-    ]
+    words = dot_nt(pick_s[64:80, :], last3[...].astype(BF16))
     given = jnp.concatenate(
-        [given[0][:, 0:lane], given[1][:, 0:lane], given[0][:, lane:], given[1][:, lane:]], axis=1
+        [words[q : q + 4, there : there + lane] for there in (0, lane) for q in (0, 4)], axis=1
     )
     gain = given[0:1] * tone[0] + given[1:2] * tone[1] + given[2:3] * tone[2]
     after = given[3:4]
@@ -527,7 +543,8 @@
         pltpu.VMEM((LANES, 2 * lanes), BF16),
         pltpu.VMEM((n, 2 * lanes), BF16),
         pltpu.VMEM((8, width // 2), F32),
-        pltpu.VMEM((32, slots), F32),
+        pltpu.VMEM((8, slots), F32),
+        pltpu.VMEM((80, LANES), BF16),
         pltpu.VMEM((width // 2, slots), F32),
         pltpu.VMEM((width // 2, slots), F32),
         pltpu.VMEM((samples, slots), F32),

time: 47.1 us -> 47.2 us (level)
  no operation moved by 1% of the time
where the time goes in v6:
time: 47.2 us; the launch traced here: 47.1 us
  Pallas kernels  46.4 us (98%)
  between operations  0.64 us (1%)
    pallas_call x1, Pallas kernels, per_device(): pl.pallas_call(functools.partial(kernel, (groups, regs, zn, rays, segs, s...  44.6 us
    pallas_call x1, Pallas kernels, per_device(): pl.pallas_call(hand_over, out_shape=shapes, in_specs=[whole] * 4, out_spe...  1.8 us

profile of v6, /device:TPU:1, one launch (start us, length us, event | category | flops | bytes accessed | tf_op | source)
XLA Modules:
  0.0 47.1 jit_solution(9746308083622746937)
XLA Ops:
  0.6 44.6 %radiance_step.1 = (f32[3,64]{1,0:T(4,128)}, bf16[1,256,256]{2,1,0:T(8,128)(2,1)}, bf16[1,2,256,256]{3,2,1,0:T(8,128)(2,1)}, bf16[4,256]{1,0:T(4,128)(2,1)}) custom-call(f32[3,64]{1,0:T(4,128)} %refs_0_.1, f32[3,64]{1,0:T(4,128)} %refs_1_.1, f32[3,64]{1,0:T(4,128)} %refs_2_.1, s32[4,64]{1,0:T(4,128)} %bitcast.10, s32[4,64]{1,0:T(4,128)} %bitcast.11, ...), custom_call_target="tpu_custom_call" | custom-call | tf_op jit(solution)/shard_map/radiance_step/pallas_call | solution.py:576
  45.3 1.8 %hand_over.1 = (f32[3,64]{1,0:T(4,128)}, bf16[1,256,256]{2,1,0:T(8,128)(2,1)}, bf16[1,2,256,256]{3,2,1,0:T(8,128)(2,1)}, bf16[4,256]{1,0:T(4,128)(2,1)}) custom-call(f32[3,64]{1,0:T(4,128)} %get-tuple-element.12.refs_0_, bf16[1,256,256]{2,1,0:T(8,128)(2,1)} %get-tuple-element.13.refs_1_, bf16[1,2,256,256]{3,2,1,0:T(8,128)(2,1)} %get-tuple-element.14.refs_2_, ...), custom_call_target="tpu_custom_call" | custom-call | tf_op jit(solution)/shard_map/hand_over/pallas_call | solution.py:587

commit v7 on v5

--- a/solution.py
+++ b/solution.py
@@ -147,32 +147,29 @@
 
 
 def direct(at, source, target, start, end_of, send, receive):
-    zn, lines = at.zn, farthest_first(at.side, at.side)
+    zn, side = at.zn, at.side
+    lines = farthest_first(side, side)
     devices = {offset: at.lines[offset] * zn for offset in lines}
     starts = {offset: start[2](*offset) for offset in lines}
     ends = {offset: end_of(*offset) for offset in lines}
-    of_core = [core * start[0] for core in at.cores]
-
-    def layer(z, nearest):
-        bases = [base + z * start[1] for base in of_core]
-        for offset in lines:
-            for core in range(at.groups - 1, -1, -1):
-                if nearest and offset == (0, 0) and core == 0:
-                    continue
-                send_part(
-                    source, target, 1, bases[core] + starts[offset], ends[offset], send, receive,
-                    (at.cores[core], devices[offset] + z),
-                )
-
-    def body(index, carry):
-        half, odd = lax.div(index, 2), lax.rem(index, 2)
-        ring = zn // 2 + half - odd * (2 * half + 1)
-        layer(lax.rem(at.z + ring, zn), False)
-        return carry
-
-    lax.fori_loop(0, zn - 1, body, 0)
-    layer(at.z, True)
-    own = of_core[0] + at.z * start[1] + starts[(0, 0)]
+    bases = {
+        (core, z): at.cores[core] * start[0] + at.layers[z] * start[1]
+        for core in range(at.groups)
+        for z in range(zn)
+    }
+    everyone = [(core, z, offset) for core, z in bases for offset in lines]
+
+    def distance(peer):
+        core, z, (y, x) = peer
+        return core + span(z, zn) + span(y, side) + span(x, side)
+
+    for core, z, offset in sorted(everyone, key=lambda peer: (-distance(peer), peer)):
+        if distance((core, z, offset)):
+            send_part(
+                source, target, 1, bases[(core, z)] + starts[offset], ends[offset], send, receive,
+                (at.cores[core], devices[offset] + at.layers[z]),
+            )
+    own = bases[(0, 0)] + starts[(0, 0)]
     target[pl.ds(ends[(0, 0)], 1), :] = source[pl.ds(own, 1), :]
     count = at.groups * at.regs - 1
     return bytes_of(source, target, count, send, receive, at.device(at.shifted(core=1)))

time: 47.1 us -> 46.9 us (level)
  no operation moved by 1% of the time
where the time goes in v7:
time: 46.9 us; the launch traced here: 46.7 us
  Pallas kernels  45.9 us (98%)
  between operations  0.8 us (2%)
    pallas_call x1, Pallas kernels, per_device(): pl.pallas_call(functools.partial(kernel, (groups, regs, zn, rays, segs, s...  44.1 us
    pallas_call x1, Pallas kernels, per_device(): pl.pallas_call(hand_over, out_shape=shapes, in_specs=[whole] * 4, out_spe...  1.78 us

profile of v7, /device:TPU:1, one launch (start us, length us, event | category | flops | bytes accessed | tf_op | source)
XLA Modules:
  0.0 46.7 jit_solution(6211796335233916658)
XLA Ops:
  0.6 44.1 %radiance_step.1 = (f32[3,64]{1,0:T(4,128)}, bf16[1,256,256]{2,1,0:T(8,128)(2,1)}, bf16[1,2,256,256]{3,2,1,0:T(8,128)(2,1)}, bf16[4,256]{1,0:T(4,128)(2,1)}) custom-call(f32[3,64]{1,0:T(4,128)} %refs_0_.1, f32[3,64]{1,0:T(4,128)} %refs_1_.1, f32[3,64]{1,0:T(4,128)} %refs_2_.1, s32[4,64]{1,0:T(4,128)} %bitcast.10, s32[4,64]{1,0:T(4,128)} %bitcast.11, ...), custom_call_target="tpu_custom_call" | custom-call | tf_op jit(solution)/shard_map/radiance_step/pallas_call | solution.py:568
  44.8 1.8 %hand_over.1 = (f32[3,64]{1,0:T(4,128)}, bf16[1,256,256]{2,1,0:T(8,128)(2,1)}, bf16[1,2,256,256]{3,2,1,0:T(8,128)(2,1)}, bf16[4,256]{1,0:T(4,128)(2,1)}) custom-call(f32[3,64]{1,0:T(4,128)} %get-tuple-element.12.refs_0_, bf16[1,256,256]{2,1,0:T(8,128)(2,1)} %get-tuple-element.13.refs_1_, bf16[1,2,256,256]{3,2,1,0:T(8,128)(2,1)} %get-tuple-element.14.refs_2_, ...), custom_call_target="tpu_custom_call" | custom-call | tf_op jit(solution)/shard_map/hand_over/pallas_call | solution.py:579

commit v8 on v7

--- a/solution.py
+++ b/solution.py
@@ -208,8 +208,6 @@
         pltpu.make_async_copy(argument, place, local.at[index])
         for index, (argument, place) in enumerate(zip(arguments, held))
     ]
-    for load in loads:
-        load.start()
     n = groups * regs
     near, far = groups * zn, regs // zn
     slots = 2 * n
@@ -227,6 +225,8 @@
     greeted += [at.shifted(y=y, x=x) for y, x in at.far_offsets()]
     for peer in greeted:
         pl.semaphore_signal(barrier, inc=1, device_id=at.device(peer), device_id_type=MESH)
+    for load in loads:
+        load.start()
     for index in (0, 1, 3, 4, 5):
         loads[index].wait()
 

time: 46.9 us -> 46.9 us (level)
  no operation moved by 1% of the time
where the time goes in v8:
time: 46.9 us; the launch traced here: 46.7 us
  Pallas kernels  45.9 us (98%)
  between operations  0.8 us (2%)
    pallas_call x1, Pallas kernels, per_device(): pl.pallas_call(functools.partial(kernel, (groups, regs, zn, rays, segs, s...  44.1 us
    pallas_call x1, Pallas kernels, per_device(): pl.pallas_call(hand_over, out_shape=shapes, in_specs=[whole] * 4, out_spe...  1.78 us

profile of v8, /device:TPU:1, one launch (start us, length us, event | category | flops | bytes accessed | tf_op | source)
XLA Modules:
  0.0 46.7 jit_solution(7860652501201963198)
XLA Ops:
  0.6 44.1 %radiance_step.1 = (f32[3,64]{1,0:T(4,128)}, bf16[1,256,256]{2,1,0:T(8,128)(2,1)}, bf16[1,2,256,256]{3,2,1,0:T(8,128)(2,1)}, bf16[4,256]{1,0:T(4,128)(2,1)}) custom-call(f32[3,64]{1,0:T(4,128)} %refs_0_.1, f32[3,64]{1,0:T(4,128)} %refs_1_.1, f32[3,64]{1,0:T(4,128)} %refs_2_.1, s32[4,64]{1,0:T(4,128)} %bitcast.10, s32[4,64]{1,0:T(4,128)} %bitcast.11, ...), custom_call_target="tpu_custom_call" | custom-call | tf_op jit(solution)/shard_map/radiance_step/pallas_call | solution.py:568
  44.8 1.8 %hand_over.1 = (f32[3,64]{1,0:T(4,128)}, bf16[1,256,256]{2,1,0:T(8,128)(2,1)}, bf16[1,2,256,256]{3,2,1,0:T(8,128)(2,1)}, bf16[4,256]{1,0:T(4,128)(2,1)}) custom-call(f32[3,64]{1,0:T(4,128)} %get-tuple-element.12.refs_0_, bf16[1,256,256]{2,1,0:T(8,128)(2,1)} %get-tuple-element.13.refs_1_, bf16[1,2,256,256]{3,2,1,0:T(8,128)(2,1)} %get-tuple-element.14.refs_2_, ...), custom_call_target="tpu_custom_call" | custom-call | tf_op jit(solution)/shard_map/hand_over/pallas_call | solution.py:579
